TPU v7x, 256 devices: a whole 4x4x8 slice. The times are simulated.
256 devices in a mesh: ctx: 8 (over y, core), head: 32 (over x, z).
Axes of the slice: x: 4, y: 4, z: 8, core: 2. Of those that a mesh axis runs over, the one named last changes fastest.
Arguments:
- queries: bfloat16 [2048, 4096], P('head'), may hold values from -102 to 102
- span_keys: bfloat16 [2048, 1024], P('head'), may hold values from -6 to 6
- span_values: bfloat16 [2048, 1024], P('head'), may hold values from -3 to 3
- cache_keys: bfloat16 [65536, 1024], P(('ctx', 'head')), may hold values from -6 to 6
- cache_values: bfloat16 [65536, 1024], P(('ctx', 'head')), may hold values from -3 to 3
- cache_lengths: int32 [16], replicated, may hold values from 1 to 16384, 65536 in all
- span_lengths: int32 [16], replicated, may hold values from 1 to 512, 2048 in all
Outputs:
- attended: bfloat16 [2048, 4096], P('head')
Inputs may be any that keep to these rules, and one draw needn't show every extreme that they name: cache_lengths sum to 65536. span_lengths sum to 2048.
All inputs are finite; a program needn't handle non-finite values.
Results may differ from a plain program's by a relative error of at most 0.0085.
The roundings to bfloat16 on the way count: a program that leaves them out, or rounds other values in their place, can miss the bound.
Values may be sent and summed in bfloat16 or wider, within the bound.
A program may use at most 192 MiB of HBM per device.

v0:
```python
import math

import jax
import jax.numpy as jnp
from jax import lax
from jax.sharding import PartitionSpec as P

H = 32
KVH = 8
HD = 128


SCORE_FLOOR = -1e30


def combined_all(value, axis, join):
    pieces = jax.tree.map(lambda part: lax.all_gather(part, axis), value)
    head = jax.tree.map(lambda part: part[0], pieces)
    tail = jax.tree.map(lambda part: part[1:], pieces)
    total, _ = lax.scan(lambda total, section: (join(total, section), None), head, tail)
    return total


def inverse_freq(head_dim):
    half_dim = head_dim // 2
    counter = jnp.arange(half_dim, dtype=jnp.float32)
    base_freq = 500000.0 ** (-2.0 * counter / head_dim)
    wavelen = 2.0 * math.pi / base_freq
    smooth = (8192.0 / wavelen - 1.0) / 3.0
    middle = (1.0 - smooth) * base_freq / 8.0 + smooth * base_freq
    return jnp.where(
        wavelen > 8192.0, base_freq / 8.0, jnp.where(wavelen < 2048.0, base_freq, middle)
    )


def rotate(vectors, positions):
    head_dim = vectors.shape[-1]
    half_dim = head_dim // 2
    angle = positions.astype(jnp.float32)[:, None] * inverse_freq(head_dim)[None, :]
    cosine = jnp.cos(angle)[:, None, :]
    sine = jnp.sin(angle)[:, None, :]
    data = vectors.astype(jnp.float32)
    lower_half = data[..., :half_dim]
    upper_half = data[..., half_dim:]
    turned = jnp.concatenate(
        [lower_half * cosine - upper_half * sine, upper_half * cosine + lower_half * sine], axis=-1
    )
    return turned.astype(jnp.bfloat16)


def lookup(doc_ids, table):
    slots = jnp.arange(table.shape[0], dtype=jnp.int32)
    return jnp.sum(jnp.where(doc_ids[:, None] == slots[None, :], table[None, :], 0), axis=1)


def documents(lengths, positions):
    ends = jnp.cumsum(lengths)
    doc_ids = jnp.sum((positions[:, None] >= ends[None, :]).astype(jnp.int32), axis=1)
    starts = ends - lengths
    return (doc_ids, positions - lookup(doc_ids, starts))


def combine(earlier, later):
    left_max, left_total, left_sum = earlier
    right_max, right_total, right_sum = later
    joint_max = jnp.maximum(left_max, right_max)
    left_factor = jnp.exp(left_max - joint_max)
    right_factor = jnp.exp(right_max - joint_max)
    joint_total = left_total * left_factor + right_total * right_factor
    joint_sum = left_sum * left_factor[..., None] + right_sum * right_factor[..., None]
    return (joint_max, joint_total, joint_sum)


def attend(query_sets, key_sets, value_sets, row_docs, row_ids, key_docs, key_ids):
    set_count, per_key, row_count, head_dim = query_sets.shape
    key_count = key_sets.shape[1]
    block_size = math.gcd(key_count, 2048)
    score_scale = 1.0 / math.sqrt(head_dim)

    def absorb(carry, start):
        run_max, run_total, run_sum = carry
        key_block = lax.dynamic_slice_in_dim(key_sets, start, block_size, 1)
        value_block = lax.dynamic_slice_in_dim(value_sets, start, block_size, 1)
        doc_block = lax.dynamic_slice_in_dim(key_docs, start, block_size, 0)
        place_block = lax.dynamic_slice_in_dim(key_ids, start, block_size, 0)
        scores = (
            jnp.einsum("kgrd,knd->kgrn", query_sets, key_block, preferred_element_type=jnp.float32)
            * score_scale
        )
        allowed = (row_docs[:, None] == doc_block[None, :]) & (
            place_block[None, :] <= row_ids[:, None]
        )
        scores = jnp.where(allowed, scores, SCORE_FLOOR)
        new_max = jnp.maximum(run_max, jnp.max(scores, axis=-1))
        weights = jnp.where(allowed, jnp.exp(scores - new_max[..., None]), 0.0)
        factor = jnp.exp(run_max - new_max)
        run_total = run_total * factor + jnp.sum(weights, axis=-1)
        run_sum = run_sum * factor[..., None] + jnp.einsum(
            "kgrn,knd->kgrd",
            weights.astype(jnp.bfloat16),
            value_block,
            preferred_element_type=jnp.float32,
        )
        return ((new_max, run_total, run_sum), None)

    state_shape = (set_count, per_key, row_count)
    start_state = (
        jnp.full(state_shape, SCORE_FLOOR, jnp.float32),
        jnp.zeros(state_shape, jnp.float32),
        jnp.zeros(state_shape + (head_dim,), jnp.float32),
    )
    starts = jnp.arange(key_count // block_size, dtype=jnp.int32) * block_size
    result, _ = lax.scan(absorb, start_state, starts)
    return result


def body(queries, span_keys, span_values, cache_keys, cache_values, cache_lengths, span_lengths):
    head_count = lax.axis_size("head")
    head_rank = lax.axis_index("head")
    ctx_rank = lax.axis_index("ctx")
    local_rows = queries.shape[0]
    row_count = local_rows * head_count
    local_tokens = cache_keys.shape[0]
    group_tokens = local_tokens * head_count
    per_group = H // KVH
    own_rows = head_rank * local_rows + jnp.arange(local_rows, dtype=jnp.int32)
    own_docs, own_offsets = documents(span_lengths, own_rows)
    own_places = lookup(own_docs, cache_lengths) + own_offsets
    token_first = (ctx_rank * head_count + head_rank) * local_tokens
    token_ids = token_first + jnp.arange(local_tokens, dtype=jnp.int32)
    token_docs, token_places = documents(cache_lengths, token_ids)
    turned_queries = rotate(queries.reshape(local_rows, H, HD), own_places)
    turned_span = rotate(span_keys.reshape(local_rows, KVH, HD), own_places)
    span_value_rows = span_values.reshape(local_rows, KVH, HD)
    turned_cache = rotate(cache_keys.reshape(local_tokens, KVH, HD), token_places)
    cache_value_rows = cache_values.reshape(local_tokens, KVH, HD)
    all_rows = jnp.arange(row_count, dtype=jnp.int32)
    all_docs, _ = documents(span_lengths, all_rows)
    group_first = ctx_rank * group_tokens

    def spread(rows_data):
        return jnp.repeat(rows_data.transpose(1, 0, 2), per_group, axis=0)

    cache_heads, cache_value_heads = (
        lax.all_to_all(spread(turned_cache), "head", split_axis=0, concat_axis=1, tiled=True),
        lax.all_to_all(spread(cache_value_rows), "head", split_axis=0, concat_axis=1, tiled=True),
    )
    query_heads, span_heads, span_value_heads = (
        lax.all_to_all(
            turned_queries.transpose(1, 0, 2), "head", split_axis=0, concat_axis=1, tiled=True
        ),
        lax.all_to_all(spread(turned_span), "head", split_axis=0, concat_axis=1, tiled=True),
        lax.all_to_all(spread(span_value_rows), "head", split_axis=0, concat_axis=1, tiled=True),
    )
    group_ids = group_first + jnp.arange(group_tokens, dtype=jnp.int32)
    group_docs, _ = documents(cache_lengths, group_ids)
    query_sets = query_heads[:, None]
    cache_part = attend(
        query_sets,
        cache_heads,
        cache_value_heads,
        all_docs,
        all_rows,
        group_docs,
        jnp.full((group_tokens,), -1, jnp.int32),
    )
    merged = combined_all(cache_part, "ctx", combine)
    span_part = attend(
        query_sets, span_heads, span_value_heads, all_docs, all_rows, all_docs, all_rows
    )
    final_max, final_total, final_sum = combine(merged, span_part)
    outputs = (final_sum / final_total[..., None]).astype(jnp.bfloat16)
    heads_here = outputs.shape[0]
    leaving = outputs.reshape(heads_here, row_count, HD).transpose(1, 0, 2)
    arrived = lax.all_to_all(leaving, "head", split_axis=0, concat_axis=1, tiled=True)
    return arrived.reshape(local_rows, H * HD)


def solution(mesh):
    placed = (
        P("head", None),
        P("head", None),
        P("head", None),
        P(("ctx", "head"), None),
        P(("ctx", "head"), None),
        P(),
        P(),
    )
    return jax.shard_map(
        body, mesh=mesh, in_specs=placed, out_specs=P("head", None), check_vma=False
    )
```

profile of v0, /device:TPU:1, one launch (start us, length us, event | category | flops | bytes accessed | tf_op | source)
XLA Modules:
  0.0 396.5 jit_solution(11907900981907821683)
XLA Ops:
  13.2 11.9 %all-to-all-start.1 = ((bf16[32,64,128]{2,1,0:T(8,128)(2,1)}), bf16[32,64,128]{2,1,0:T(8,128)(2,1)S(1)}, u32[]{:S(2)}, u32[]{:S(2)}) async-start(bf16[32,64,128]{2,1,0:T(8,128)(2,1)} %maximum_bitcast_fusion.1), calls=%async_computation.1 | async-start | bytes 1048576 | tf_op jit(solution)/shard_map/all_to_all | solution.py:149
  29.6 9.8 %all-to-all-done.1 = bf16[32,64,128]{2,1,0:T(8,128)(2,1)S(1)} async-done(((bf16[32,64,128]{2,1,0:T(8,128)(2,1)}), bf16[32,64,128]{2,1,0:T(8,128)(2,1)S(1)}, u32[]{:S(2)}, u32[]{:S(2)}) %all-to-all-start.1) | async-done | bytes 524320 | tf_op jit(solution)/shard_map/all_to_all | solution.py:149
  41.3 7.5 %all-to-all-start = ((bf16[32,256,128]{2,1,0:T(8,128)(2,1)}), bf16[32,256,128]{2,1,0:T(8,128)(2,1)S(1)}, u32[]{:S(2)}, u32[]{:S(2)}) async-start(bf16[32,256,128]{2,1,0:T(8,128)(2,1)} %bitcast.8), calls=%async_computation | async-start | bytes 4194304 | tf_op jit(solution)/shard_map/all_to_all | solution.py:145
  49.0 49.2 %all-to-all-done = bf16[32,256,128]{2,1,0:T(8,128)(2,1)S(1)} async-done(((bf16[32,256,128]{2,1,0:T(8,128)(2,1)}), bf16[32,256,128]{2,1,0:T(8,128)(2,1)S(1)}, u32[]{:S(2)}, u32[]{:S(2)}) %all-to-all-start) | async-done | bytes 2097184 | tf_op jit(solution)/shard_map/all_to_all | solution.py:145
  106.8 48.3 %all-to-all-done.2 = bf16[32,256,128]{2,1,0:T(8,128)(2,1)} async-done(((bf16[32,256,128]{2,1,0:T(8,128)(2,1)}), bf16[32,256,128]{2,1,0:T(8,128)(2,1)}, u32[]{:S(2)}, u32[]{:S(2)}) %all-to-all-start.2) | async-done | bytes 2097184 | tf_op jit(solution)/shard_map/all_to_all | solution.py:146
  155.1 98.2 %while.36 = (s32[]{:T(128)}, f32[1,1,2048]{2,1,0:T(1,128)S(1)}, f32[1,1,2048]{2,1,0:T(1,128)S(1)}, f32[1,1,2048,128]{3,2,1,0:T(8,128)}, s32[2048]{0:T(1024)S(1)}...) while((s32[]{:T(128)}, f32[1,1,2048]{2,1,0:T(1,128)S(1)}, ...), condition=%wide.region_12.13_spmd.clone, body=%wide.region_9.12_spmd.clone.sunk | while | flops 2227974144 | bytes 62595328 | solution.py:113
  163.2 7.0 %fusion.83 = f32[2048]{0:T(1024)S(1)} fusion(f32[2048]{0:T(1024)S(1)} %bitcast.164, f32[2048,2048]{1,0:T(8,128)S(1)} %get-tuple-element.393, pred[2048]{0:T(1024)(128)(4,1)S(1)} %iota_compare_fusion.6, s32[2048]{0:T(1024)S(1)} %dynamic_slice.66, s32[2048]{0:T(1024)S(1)} %get-tuple-element.426), kind=kLoop, calls=%fused_computation.15.clone.1 | loop fusion | flops 29358080 | bytes 16812032 | tf_op jit(solution)/shard_map/while/body/eval_jaxpr/reduce_sum | solution.py:97
  170.3 8.3 %fusion.85 = f32[1,1,2048,128]{3,2,1,0:T(8,128)S(1)} fusion(f32[2048]{0:T(1024)S(1)} %bitcast.165, f32[2048,2048]{1,0:T(8,128)S(1)} %get-tuple-element.393, pred[2048]{0:T(1024)(128)(4,1)S(1)} %iota_compare_fusion.6, s32[2048]{0:T(1024)S(1)} %dynamic_slice.66, s32[2048]{0:T(1024)S(1)} %get-tuple-element.426, f32[1,1,2048,128]{3,2,1,0:T(8,128)S(1)} %copy-done.1, ...), kind=kOutput, calls=%fused_computation.17.clone.1 | convolution fusion | flops 1103888384 | bytes 19433476 | tf_op jit(solution)/shard_map/while/body/eval_jaxpr/kgrn,knd->kgrd/dot_general | solution.py:98
  187.8 7.0 %fusion.83 = f32[2048]{0:T(1024)S(1)} fusion(f32[2048]{0:T(1024)S(1)} %bitcast.164, f32[2048,2048]{1,0:T(8,128)S(1)} %get-tuple-element.393, pred[2048]{0:T(1024)(128)(4,1)S(1)} %iota_compare_fusion.6, s32[2048]{0:T(1024)S(1)} %dynamic_slice.66, s32[2048]{0:T(1024)S(1)} %get-tuple-element.426), kind=kLoop, calls=%fused_computation.15.clone.1 | loop fusion | flops 29358080 | bytes 16812032 | tf_op jit(solution)/shard_map/while/body/eval_jaxpr/reduce_sum | solution.py:97
  194.9 8.3 %fusion.85 = f32[1,1,2048,128]{3,2,1,0:T(8,128)S(1)} fusion(f32[2048]{0:T(1024)S(1)} %bitcast.165, f32[2048,2048]{1,0:T(8,128)S(1)} %get-tuple-element.393, pred[2048]{0:T(1024)(128)(4,1)S(1)} %iota_compare_fusion.6, s32[2048]{0:T(1024)S(1)} %dynamic_slice.66, s32[2048]{0:T(1024)S(1)} %get-tuple-element.426, f32[1,1,2048,128]{3,2,1,0:T(8,128)S(1)} %copy-done.1, ...), kind=kOutput, calls=%fused_computation.17.clone.1 | convolution fusion | flops 1103888384 | bytes 19433476 | tf_op jit(solution)/shard_map/while/body/eval_jaxpr/kgrn,knd->kgrd/dot_general | solution.py:98
  212.3 7.0 %fusion.83 = f32[2048]{0:T(1024)S(1)} fusion(f32[2048]{0:T(1024)S(1)} %bitcast.164, f32[2048,2048]{1,0:T(8,128)S(1)} %get-tuple-element.393, pred[2048]{0:T(1024)(128)(4,1)S(1)} %iota_compare_fusion.6, s32[2048]{0:T(1024)S(1)} %dynamic_slice.66, s32[2048]{0:T(1024)S(1)} %get-tuple-element.426), kind=kLoop, calls=%fused_computation.15.clone.1 | loop fusion | flops 29358080 | bytes 16812032 | tf_op jit(solution)/shard_map/while/body/eval_jaxpr/reduce_sum | solution.py:97
  219.4 8.3 %fusion.85 = f32[1,1,2048,128]{3,2,1,0:T(8,128)S(1)} fusion(f32[2048]{0:T(1024)S(1)} %bitcast.165, f32[2048,2048]{1,0:T(8,128)S(1)} %get-tuple-element.393, pred[2048]{0:T(1024)(128)(4,1)S(1)} %iota_compare_fusion.6, s32[2048]{0:T(1024)S(1)} %dynamic_slice.66, s32[2048]{0:T(1024)S(1)} %get-tuple-element.426, f32[1,1,2048,128]{3,2,1,0:T(8,128)S(1)} %copy-done.1, ...), kind=kOutput, calls=%fused_computation.17.clone.1 | convolution fusion | flops 1103888384 | bytes 19433476 | tf_op jit(solution)/shard_map/while/body/eval_jaxpr/kgrn,knd->kgrd/dot_general | solution.py:98
  236.9 7.0 %fusion.83 = f32[2048]{0:T(1024)S(1)} fusion(f32[2048]{0:T(1024)S(1)} %bitcast.164, f32[2048,2048]{1,0:T(8,128)S(1)} %get-tuple-element.393, pred[2048]{0:T(1024)(128)(4,1)S(1)} %iota_compare_fusion.6, s32[2048]{0:T(1024)S(1)} %dynamic_slice.66, s32[2048]{0:T(1024)S(1)} %get-tuple-element.426), kind=kLoop, calls=%fused_computation.15.clone.1 | loop fusion | flops 29358080 | bytes 16812032 | tf_op jit(solution)/shard_map/while/body/eval_jaxpr/reduce_sum | solution.py:97
  243.9 8.3 %fusion.85 = f32[1,1,2048,128]{3,2,1,0:T(8,128)S(1)} fusion(f32[2048]{0:T(1024)S(1)} %bitcast.165, f32[2048,2048]{1,0:T(8,128)S(1)} %get-tuple-element.393, pred[2048]{0:T(1024)(128)(4,1)S(1)} %iota_compare_fusion.6, s32[2048]{0:T(1024)S(1)} %dynamic_slice.66, s32[2048]{0:T(1024)S(1)} %get-tuple-element.426, f32[1,1,2048,128]{3,2,1,0:T(8,128)S(1)} %copy-done.1, ...), kind=kOutput, calls=%fused_computation.17.clone.1 | convolution fusion | flops 1103888384 | bytes 19433476 | tf_op jit(solution)/shard_map/while/body/eval_jaxpr/kgrn,knd->kgrd/dot_general | solution.py:98
  254.6 7.0 %all-to-all-start.3 = ((bf16[32,64,128]{2,1,0:T(8,128)(2,1)}), bf16[32,64,128]{2,1,0:T(8,128)(2,1)S(1)}, u32[]{:S(2)}, u32[]{:S(2)}) async-start(bf16[32,64,128]{2,1,0:T(8,128)(2,1)} %bitcast.23), calls=%async_computation.3 | async-start | bytes 1048576 | tf_op jit(solution)/shard_map/all_to_all | solution.py:152
  261.7 13.7 %all-to-all-done.3 = bf16[32,64,128]{2,1,0:T(8,128)(2,1)S(1)} async-done(((bf16[32,64,128]{2,1,0:T(8,128)(2,1)}), bf16[32,64,128]{2,1,0:T(8,128)(2,1)S(1)}, u32[]{:S(2)}, u32[]{:S(2)}) %all-to-all-start.3) | async-done | bytes 524320 | tf_op jit(solution)/shard_map/all_to_all | solution.py:152
  276.3 7.9 %all-to-all-start.4 = ((bf16[32,64,128]{2,1,0:T(8,128)(2,1)}), bf16[32,64,128]{2,1,0:T(8,128)(2,1)S(1)}, u32[]{:S(2)}, u32[]{:S(2)}) async-start(bf16[32,64,128]{2,1,0:T(8,128)(2,1)} %bitcast.28), calls=%async_computation.4 | async-start | bytes 1048576 | tf_op jit(solution)/shard_map/all_to_all | solution.py:153
  294.5 7.1 %fusion.31 = f32[2048]{0:T(1024)S(1)} fusion(f32[2048,2048]{0,1:T(8,128)S(1)} %get-tuple-element.275, f32[2048]{0:T(1024)S(1)} %get-tuple-element.269, s32[2048]{0:T(1024)S(1)} %get-tuple-element.468), kind=kLoop, calls=%fused_computation.42 | loop fusion | flops 33552384 | bytes 16801792 | tf_op jit(solution)/shard_map/while/body/eval_jaxpr/reduce_sum | solution.py:97
  301.6 14.7 %all-gather = f32[8,1,2048]{2,1,0:T(1,128)S(1)} all-gather(f32[1,1,2048]{2,1,0:T(1,128)S(1)} %get-tuple-element.130), channel_id=2, replica_groups=mesh['ctx'=8,'head'=32] {'ctx'}, dimensions={0}, use_global_device_ids=true | all-gather | bytes 73728 | tf_op jit(solution)/shard_map/all_gather | solution.py:17
  316.4 12.7 %all-gather.1 = f32[8,1,2048]{2,1,0:T(1,128)S(1)} all-gather(f32[1,1,2048]{2,1,0:T(1,128)S(1)} %get-tuple-element.131), channel_id=3, replica_groups=mesh['ctx'=8,'head'=32] {'ctx'}, dimensions={0}, use_global_device_ids=true | all-gather | bytes 73728 | tf_op jit(solution)/shard_map/all_gather | solution.py:17
  329.2 6.6 %slice_bitcast_fusion = f32[7,1,1,2048,128]{4,3,2,1,0:T(8,128)} fusion(f32[8,1,2048,128]{3,2,1,0:T(8,128)} %all-gather.5.cloned.1.call-done), kind=kLoop, calls=%fused_computation.45 | loop fusion | bytes 14680064 | tf_op jit(solution)/shard_map/while | solution.py:20
  335.8 15.1 %while.11 = (s32[]{:T(128)}, f32[1,1,2048]{2,1,0:T(1,128)S(1)}, f32[1,1,2048]{2,1,0:T(1,128)S(1)}, f32[1,1,2048,128]{3,2,1,0:T(8,128)S(1)}, f32[7,1,1,2048]{3,2,...) while((s32[]{:T(128)}, f32[1,1,2048]{2,1,0:T(1,128)S(1)}, ...), condition=%wide.region_14.15_spmd, body=%wide.region_13.14_spmd.sunk | while | flops 798722 | bytes 3227749 | solution.py:20
  350.9 11.1 %fusion.53 = bf16[2048,1,128]{2,0,1:T(8,128)(2,1)S(1)} fusion(bf16[2048,128]{1,0:T(8,128)(2,1)S(1)} %bitcast.177, f32[2048,2048]{0,1:T(8,128)} %copy-done, f32[2048]{0:T(1024)S(1)} %get-tuple-element.269, s32[2048]{0:T(1024)S(1)} %get-tuple-element.468, f32[1,1,2048,128]{3,2,1,0:T(8,128)S(1)} %get-tuple-element.133, f32[2048]{0:T(1024)S(1)} %bitcast.185, ...), kind=kOutput, calls=%fused_computation.52 | convolution fusion | flops 1108869120 | bytes 18923520 | tf_op jit(solution)/shard_map/while/body/eval_jaxpr/kgrn,knd->kgrd/dot_general | solution.py:98
  363.7 24.0 %all_to_all.66 = bf16[32,2,4096]{2,1,0:T(2,128)(2,1)S(1)} all-to-all(bf16[32,2,4096]{2,1,0:T(2,128)(2,1)S(1)} %reshape.432), channel_id=1, replica_groups=mesh['ctx'=8,'head'=32] {'head'}, dimensions={0} | all-to-all | bytes 1048576 | tf_op jit(solution)/shard_map/all_to_all | solution.py:175
  (138 shorter events, 82.3 us)
Async XLA Ops:
  6.5 42.3 %copy-start.3 = (bf16[256,1024]{1,0:T(8,128)(2,1)S(1)}, bf16[256,1024]{1,0:T(8,128)(2,1)}, u32[]{:S(2)}) copy-start(bf16[256,1024]{1,0:T(8,128)(2,1)} %param.15) | copy-start | bytes 1572868
  13.2 26.2 %all-to-all-start.1 = ((bf16[32,64,128]{2,1,0:T(8,128)(2,1)}), bf16[32,64,128]{2,1,0:T(8,128)(2,1)S(1)}, u32[]{:S(2)}, u32[]{:S(2)}) async-start(bf16[32,64,128]{2,1,0:T(8,128)(2,1)} %maximum_bitcast_fusion.1), calls=%async_computation.1 | async-start | bytes 1048576 | tf_op jit(solution)/shard_map/all_to_all | solution.py:149
  39.4 1.9 copy-start.4
  41.3 56.9 %all-to-all-start = ((bf16[32,256,128]{2,1,0:T(8,128)(2,1)}), bf16[32,256,128]{2,1,0:T(8,128)(2,1)S(1)}, u32[]{:S(2)}, u32[]{:S(2)}) async-start(bf16[32,256,128]{2,1,0:T(8,128)(2,1)} %bitcast.8), calls=%async_computation | async-start | bytes 4194304 | tf_op jit(solution)/shard_map/all_to_all | solution.py:145
  100.0 55.1 %all-to-all-start.2 = ((bf16[32,256,128]{2,1,0:T(8,128)(2,1)}), bf16[32,256,128]{2,1,0:T(8,128)(2,1)}, u32[]{:S(2)}, u32[]{:S(2)}) async-start(bf16[32,256,128]{2,1,0:T(8,128)(2,1)} %bitcast.13), calls=%async_computation.2 | async-start | bytes 4194304 | tf_op jit(solution)/shard_map/all_to_all | solution.py:146
  106.5 222.7 %all-gather.5.cloned.1.call-start = ((), (), s32[]{:S(2)}) async-start(), calls=%async_computation.6 | async-start | bytes 9437184 | tf_op jit(solution)/shard_map/all_gather | solution.py:17
  155.1 98.2 %copy-start.5 = (bf16[64,1024]{1,0:T(8,128)(2,1)S(1)}, bf16[64,1024]{1,0:T(8,128)(2,1)}, u32[]{:S(2)}) copy-start(bf16[64,1024]{1,0:T(8,128)(2,1)} %param.12) | copy-start | bytes 393220
  155.1 106.5 %copy-start.6 = (bf16[64,1024]{1,0:T(8,128)(2,1)S(1)}, bf16[64,1024]{1,0:T(8,128)(2,1)}, u32[]{:S(2)}) copy-start(bf16[64,1024]{1,0:T(8,128)(2,1)} %param.13) | copy-start | bytes 393220
  157.7 12.6 %copy-start.1 = (f32[1,1,2048,128]{3,2,1,0:T(8,128)S(1)}, f32[1,1,2048,128]{3,2,1,0:T(8,128)}, u32[]{:S(2)}) copy-start(f32[1,1,2048,128]{3,2,1,0:T(8,128)} %get-tuple-element.412) | copy-start | bytes 3145732 | tf_op jit(solution)/shard_map/while
  178.6 1.1 copy-start.2
  182.2 12.6 %copy-start.1 = (f32[1,1,2048,128]{3,2,1,0:T(8,128)S(1)}, f32[1,1,2048,128]{3,2,1,0:T(8,128)}, u32[]{:S(2)}) copy-start(f32[1,1,2048,128]{3,2,1,0:T(8,128)} %get-tuple-element.412) | copy-start | bytes 3145732 | tf_op jit(solution)/shard_map/while
  203.1 1.1 copy-start.2
  206.7 12.6 %copy-start.1 = (f32[1,1,2048,128]{3,2,1,0:T(8,128)S(1)}, f32[1,1,2048,128]{3,2,1,0:T(8,128)}, u32[]{:S(2)}) copy-start(f32[1,1,2048,128]{3,2,1,0:T(8,128)} %get-tuple-element.412) | copy-start | bytes 3145732 | tf_op jit(solution)/shard_map/while
  227.7 1.1 copy-start.2
  231.3 12.6 %copy-start.1 = (f32[1,1,2048,128]{3,2,1,0:T(8,128)S(1)}, f32[1,1,2048,128]{3,2,1,0:T(8,128)}, u32[]{:S(2)}) copy-start(f32[1,1,2048,128]{3,2,1,0:T(8,128)} %get-tuple-element.412) | copy-start | bytes 3145732 | tf_op jit(solution)/shard_map/while
  252.2 1.1 copy-start.2
  254.6 20.7 %all-to-all-start.3 = ((bf16[32,64,128]{2,1,0:T(8,128)(2,1)}), bf16[32,64,128]{2,1,0:T(8,128)(2,1)S(1)}, u32[]{:S(2)}, u32[]{:S(2)}) async-start(bf16[32,64,128]{2,1,0:T(8,128)(2,1)} %bitcast.23), calls=%async_computation.3 | async-start | bytes 1048576 | tf_op jit(solution)/shard_map/all_to_all | solution.py:152
  276.3 74.6 %all-to-all-start.4 = ((bf16[32,64,128]{2,1,0:T(8,128)(2,1)}), bf16[32,64,128]{2,1,0:T(8,128)(2,1)S(1)}, u32[]{:S(2)}, u32[]{:S(2)}) async-start(bf16[32,64,128]{2,1,0:T(8,128)(2,1)} %bitcast.28), calls=%async_computation.4 | async-start | bytes 1048576 | tf_op jit(solution)/shard_map/all_to_all | solution.py:153
  288.6 5.9 %copy-start = (f32[2048,2048]{0,1:T(8,128)}, f32[2048,2048]{0,1:T(8,128)S(1)}, u32[]{:S(2)}) copy-start(f32[2048,2048]{0,1:T(8,128)S(1)} %get-tuple-element.275) | copy-start | bytes 50331652
  329.1 6.7 %slice-start = ((f32[8,1,2048,128]{3,2,1,0:T(8,128)}), f32[1,1,2048,128]{3,2,1,0:T(8,128)S(1)}, s32[]{:S(2)}) async-start(f32[8,1,2048,128]{3,2,1,0:T(8,128)} %all-gather.5.cloned.1.call-done), calls=%async_computation.7 | async-start | bytes 2097152 | tf_op jit(solution)/shard_map/slice | solution.py:18
Sparse Core Ops, SparseCore 0:
  253.4 52.1 all-gather.4
where the time goes:
time: 400 us; the launch traced here: 396 us
  waiting for transfers between devices  121 us (30%)
  matrix products  70.8 us (18%)
  other arithmetic  60.8 us (15%)
  blocking collectives  51.4 us (13%)
  starting transfers between devices  40.8 us (10%)
  local copies, waits for them, and re-layouts  30.2 us (8%)
  between operations  13.8 us (3%)
  loops' own time  7.8 us (2%)
    all_to_all x1, waiting for transfers between devices, body(): lax.all_to_all(spread(turned_cache), 'head', split_axis=0, concat_axis=1,...  49.2 us
    all_to_all x1, waiting for transfers between devices, body(): lax.all_to_all(spread(cache_value_rows), 'head', split_axis=0, concat_axi...  48.3 us
    dot_general x5, matrix products, absorb(): jnp.einsum('kgrn,knd->kgrd', weights.astype(jnp.bfloat16), value_block, p...  44.2 us
    reduce_sum x5, other arithmetic, absorb(): run_total = run_total * factor + jnp.sum(weights, axis=-1)  35.2 us
    all_gather x2, blocking collectives, combined_all(): pieces = jax.tree.map(lambda part: lax.all_gather(part, axis), value)  27.5 us
    dot_general x5, matrix products, absorb(): jnp.einsum('kgrd,knd->kgrn', query_sets, key_block, preferred_element_typ...  26.5 us
    all_to_all x1, blocking collectives, body(): lax.all_to_all(leaving, 'head', split_axis=0, concat_axis=1, tiled=True)  24 us
    add x7, other arithmetic, combine(): left_sum * left_factor[..., None] + right_sum * right_factor[..., None]  14.6 us
  transfers between devices with their start and end apart: 6, of which 4 were waited for; matrix products, arithmetic and copies ran while one was open for 10% of the time, Pallas kernels for 0%

commit v1 on v0

v1 whole, which is shorter than its diff:
```python
import functools
import math

import jax
import jax.numpy as jnp
import numpy as np
from jax import lax
from jax.experimental import pallas as pl
from jax.experimental.pallas import tpu as pltpu
from jax.sharding import PartitionSpec as P

HD = 128
GROUP = 4
X = 4
FLOOR = -1e30
MESH = pl.DeviceIdType.MESH
VMEM = pltpu.VMEM
SCALE = math.log2(math.e) / math.sqrt(HD)


def inverse_freq():
    counter = np.arange(HD // 2, dtype=np.float64)
    base = 500000.0 ** (-2.0 * counter / HD)
    wavelen = 2.0 * math.pi / base
    smooth = (8192.0 / wavelen - 1.0) / 3.0
    middle = (1.0 - smooth) * base / 8.0 + smooth * base
    freq = np.where(wavelen > 8192.0, base / 8.0, np.where(wavelen < 2048.0, base, middle))
    return np.concatenate([freq, freq]).astype(np.float32)[None, :]


class Place:
    def __init__(self, ctx_size, head_size):
        self.Y = ctx_size // 2
        self.Z = head_size // X
        ctx = lax.axis_index("ctx")
        head = lax.axis_index("head")
        self.ctx, self.head = ctx, head
        self.y = ctx // 2
        self.c = ctx % 2
        self.x = head // self.Z
        self.z = head % self.Z
        self.pair = self.x // 2
        self.hb = self.bit_of(self.x)
        self.k = 2 * self.y + self.hb
        self.sgn = 1 - 2 * self.c

    def bit_of(self, x):
        pair = x // 2
        return pair * 3 + x * (1 - 2 * pair)

    def dev(self, y=None, c=None, x=None, z=None):
        y = self.y if y is None else y
        c = self.c if c is None else c
        x = self.x if x is None else x
        z = self.z if z is None else z
        return (y * 2 + c, x * self.Z + z)

    def z_at(self, offset):
        return (self.z + self.sgn * offset + 2 * self.Z) % self.Z

    def along_z(self, offset):
        return self.dev(z=self.z_at(offset))

    def key_partner(self, d):
        k = (self.k + d) % (2 * self.Y)
        hb = k % 2
        x = self.pair * 3 + hb * (1 - 2 * self.pair)
        return k, self.dev(y=k // 2, x=x)


def barrier(devices):
    sem = pltpu.get_barrier_semaphore()
    for device in devices:
        pl.semaphore_signal(sem, inc=1, device_id=device, device_id_type=MESH)
    pl.semaphore_wait(sem, len(devices))


def remote(src, dst, send, recv, device):
    return pltpu.make_async_remote_copy(
        src_ref=src, dst_ref=dst, send_sem=send, recv_sem=recv, device_id=device, device_id_type=MESH
    )


def turn(data, cosine, sine):
    data = data.astype(jnp.float32)
    return (data * cosine + pltpu.roll(data, HD // 2, 1) * sine).astype(jnp.bfloat16)


def trig(place, freq):
    angle = place.astype(jnp.float32) * freq
    lane = lax.broadcasted_iota(jnp.int32, angle.shape, 1)
    sine = jnp.sin(angle)
    return jnp.cos(angle), jnp.where(lane < HD // 2, -sine, sine)


def ring_hops(Z):
    near, far = Z // 2 - 1, Z // 2
    hops = []
    for step in range(far):
        hops.append((0, step))
        if step < near:
            hops.append((1, step))
    return hops


def gather_kernel(
    sizes, cl, sl, freq_ref, q_ref, sk_ref, sv_ref, k_ref, v_ref,
    qo, ko, vo, sko, svo,
    q_in, sk_in, qs, sks, ks,
    q_in_sem, span_sem, v_send, v_recv, k_send, k_recv, x_send, x_recv, ring_send, ring_recv,
    core_send, core_recv, own_sem, pair_send, pair_recv,
):
    at = Place(*sizes)
    Y, Z = at.Y, at.Z
    heads = 2 * Y
    rows, tokens = q_ref.shape[0], k_ref.shape[0]
    ndoc = cl.shape[0]

    reads = []
    for hb in range(2):
        column = pl.multiple_of((2 * at.y + hb) * (GROUP * HD) + at.c * (2 * HD), 2 * HD)
        reads.append(
            pltpu.make_async_copy(q_ref.at[:, pl.ds(column, 2 * HD)], q_in.at[hb], q_in_sem.at[hb])
        )
    own = pl.multiple_of(at.k * HD, HD)
    theirs = pl.multiple_of((at.k + 1 - 2 * at.hb) * HD, HD)
    for i, column in enumerate((own, theirs)):
        reads.append(
            pltpu.make_async_copy(sk_ref.at[:, pl.ds(column, HD)], sk_in.at[i], span_sem.at[i])
        )
    for copy in reads:
        copy.start()
    sv_copy = pltpu.make_async_copy(sv_ref.at[:, pl.ds(own, HD)], svo.at[0], span_sem.at[2])
    sv_copy.start()
    v_own = pltpu.make_async_copy(v_ref.at[:, pl.ds(own, HD)], vo.at[at.k], own_sem.at[0])
    v_own.start()

    partners = [at.key_partner(d) for d in range(1, heads)]
    others = [at.dev(x=(at.x + dx) % X) for dx in range(1, X)]
    plus, minus = at.along_z(1), at.along_z(-1)
    other_core = at.dev(c=1 - at.c)
    outside = [at.dev(x=(at.x + 2) % X), at.dev(x=3 - at.x)]
    greet = [device for _, device in partners] + outside + [other_core, plus]
    if Z > 2:
        greet.append(minus)
    barrier(greet)

    order = sorted(range(1, heads), key=lambda d: -min(d, heads - d))
    v_copies = []
    for d in order:
        k, device = partners[d - 1]
        column = pl.multiple_of(k * HD, HD)
        copy = remote(
            v_ref.at[:, pl.ds(column, HD)], vo.at[at.k], v_send.at[d], v_recv.at[d], device
        )
        copy.start()
        v_copies.append(copy)

    freq = freq_ref[...]
    row = at.head * rows + lax.broadcasted_iota(jnp.int32, (rows, HD), 0)
    shift = jnp.zeros((rows, HD), jnp.int32)
    start = jnp.int32(0)
    for d in range(ndoc):
        shift = jnp.where(row >= start, cl[d] - start, shift)
        start = start + sl[d]
    cosine, sine = trig(row + shift, freq)
    for copy in reads:
        copy.wait()
    for hb in range(2):
        for h in range(2):
            qs[hb, h * rows : (h + 1) * rows, :] = turn(
                q_in[hb, :, h * HD : (h + 1) * HD], cosine, sine
            )
    sko[0] = turn(sk_in[0], cosine, sine)
    sks[...] = turn(sk_in[1], cosine, sine)

    x_copies = []
    for dx in range(1, X):
        x = (at.x + dx) % X
        copy = remote(
            qs.at[at.bit_of(x)], qo.at[at.c, at.z, at.x], x_send.at[dx], x_recv.at[dx], others[dx - 1]
        )
        copy.start()
        x_copies.append(copy)
    mate = at.dev(x=at.pair * 3 + (1 - at.hb) * (1 - 2 * at.pair))
    pair_copies = [
        remote(sks, sko.at[1], pair_send.at[0], pair_recv.at[0], mate),
        remote(sv_ref.at[:, pl.ds(theirs, HD)], svo.at[1], pair_send.at[1], pair_recv.at[1], mate),
    ]
    for copy in pair_copies:
        copy.start()
    q_own = pltpu.make_async_copy(qs.at[at.hb], qo.at[at.c, at.z, at.x], own_sem.at[1])
    q_own.start()

    def ring_copy(direction, step, n):
        offset = -step if direction == 0 else step
        x = (at.x - n + X) % X
        part = qo.at[at.c, at.z_at(offset), x]
        return remote(
            part, part, ring_send.at[direction, step, n], ring_recv.at[direction, step, n],
            plus if direction == 0 else minus,
        )

    def arrived(direction, step, n):
        offset = -(step + 1) if direction == 0 else step + 1
        x = (at.x - n + X) % X
        part = qo.at[at.c, at.z_at(offset), x]
        remote(
            part, part, ring_send.at[direction, step, n], ring_recv.at[direction, step, n], plus
        ).wait_recv()

    def core_copy(i, offset):
        slab = qo.at[at.c, at.z_at(offset)]
        return remote(slab, slab, core_send.at[i], core_recv.at[i], other_core)

    hops = ring_hops(Z)
    ring = []
    for n in range(X):
        if n == 0:
            q_own.wait()
        else:
            x_copies[n - 1].wait_recv()
        for direction in range(2):
            if (direction, 0) in hops:
                copy = ring_copy(direction, 0, n)
                copy.start()
                ring.append(copy)
    cores = [core_copy(0, 0)]
    cores[0].start()

    token = (at.ctx * sizes[1] + at.head) * tokens + lax.broadcasted_iota(jnp.int32, (tokens, HD), 0)
    first = jnp.zeros((tokens, HD), jnp.int32)
    start = jnp.int32(0)
    for d in range(ndoc):
        first = jnp.where(token >= start, start, first)
        start = start + cl[d]
    cosine, sine = trig(token - first, freq)
    k_copies = []
    for d in order:
        k, device = partners[d - 1]
        column = pl.multiple_of(k * HD, HD)
        ks[d - 1] = turn(k_ref[:, pl.ds(column, HD)], cosine, sine)
        copy = remote(ks.at[d - 1], ko.at[at.k], k_send.at[d], k_recv.at[d], device)
        copy.start()
        k_copies.append(copy)
    ko[at.k] = turn(k_ref[:, pl.ds(own, HD)], cosine, sine)

    for i, (direction, step) in enumerate(hops):
        onward = (direction, step + 1) in hops
        for n in range(X):
            arrived(direction, step, n)
            if onward:
                copy = ring_copy(direction, step + 1, n)
                copy.start()
                ring.append(copy)
        copy = core_copy(i + 1, -(step + 1) if direction == 0 else step + 1)
        copy.start()
        cores.append(copy)

    for i in range(Z):
        if i == 0:
            offset = 0
        else:
            direction, step = hops[i - 1]
            offset = (step + 1) if direction == 0 else -(step + 1)
        slab = qo.at[1 - at.c, at.z_at(offset)]
        remote(slab, slab, core_send.at[i], core_recv.at[i], other_core).wait_recv()
    for copy in v_copies + k_copies + pair_copies:
        copy.wait_recv()
    for copy in v_copies + k_copies + pair_copies + x_copies + ring + cores:
        copy.wait_send()
    v_own.wait()
    sv_copy.wait()


def attend_kernel(sizes, cl, sl, q_ref, k_ref, v_ref, sk_ref, sv_ref, part_ref, stat_ref, acc):
    at = Place(*sizes)
    Z = at.Z
    blocks, tokens, _ = k_ref.shape
    rows = q_ref.shape[3] // 2
    lanes = 4 * rows
    ndoc = cl.shape[0]

    half = lax.broadcasted_iota(jnp.int32, (2, Z, 2 * X, 2 * rows), 2)
    stat_ref[...] = jnp.where(half < X, FLOOR, 0.0)
    acc[...] = jnp.zeros_like(acc)
    lane = lax.broadcasted_iota(jnp.int32, (1, lanes), 1) % rows

    def absorb(keys, values_t, n, row_low, row_high, masked):
        x, z = n // Z, n % Z
        q = jnp.concatenate([q_ref[0, z, x], q_ref[1, z, x]], axis=0)
        s = lax.dot_general(
            keys, q, (((1,), (1,)), ((), ())), preferred_element_type=jnp.float32
        )
        row = n * rows + lane
        s = masked(s * SCALE, row)
        m_old = jnp.concatenate(
            [stat_ref[0, z, pl.ds(x, 1), :], stat_ref[1, z, pl.ds(x, 1), :]], axis=1
        )
        l_old = jnp.concatenate(
            [stat_ref[0, z, pl.ds(X + x, 1), :], stat_ref[1, z, pl.ds(X + x, 1), :]], axis=1
        )
        here = (row >= row_low) & (row < row_high)
        m_new = jnp.where(here, jnp.maximum(m_old, jnp.max(s, axis=0, keepdims=True)), m_old)
        w = jnp.exp2(s - jnp.where(here, m_new, -FLOOR))
        factor = jnp.exp2(m_old - m_new)
        l_new = l_old * factor + jnp.sum(w, axis=0, keepdims=True)
        o = jnp.dot(values_t, w.astype(jnp.bfloat16), preferred_element_type=jnp.float32)
        for c in range(2):
            part = slice(c * 2 * rows, (c + 1) * 2 * rows)
            stat_ref[c, z, pl.ds(x, 1), :] = m_new[:, part]
            stat_ref[c, z, pl.ds(X + x, 1), :] = l_new[:, part]
            acc[c, z, x] = acc[c, z, x] * factor[:, part] + o[:, part]

    def block_step(b, carry):
        first = (((b // 2) * 2 + at.c) * sizes[1] + (at.pair * 3 + (b % 2) * (1 - 2 * at.pair)) * Z + at.z) * tokens
        keys = k_ref[b]
        values_t = v_ref[b].T
        token = first + lax.broadcasted_iota(jnp.int32, (tokens, lanes), 0)

        def doc_step(d, carry):
            cache_start, span_start = carry
            cache_end, span_end = cache_start + cl[d], span_start + sl[d]
            overlap = (cache_end > first) & (cache_start < first + tokens)

            def masked(s, row):
                return jnp.where((token >= cache_start) & (token < cache_end), s, FLOOR)

            def chunk(n, carry):
                absorb(keys, values_t, n, span_start, span_end, masked)
                return carry

            low = span_start // rows
            high = jnp.where(overlap, (span_end + rows - 1) // rows, low)
            lax.fori_loop(low, high, chunk, 0)
            return cache_end, span_end

        lax.fori_loop(0, ndoc, doc_step, (jnp.int32(0), jnp.int32(0)))
        return carry

    lax.fori_loop(0, blocks, block_step, 0)

    mate = at.pair * 3 + (1 - at.hb) * (1 - 2 * at.pair)
    own_chunk = jnp.where(at.c == 0, at.x, mate) * Z + at.z
    first = own_chunk * rows
    keys = sk_ref[at.c]
    values_t = sv_ref[at.c].T
    token = first + lax.broadcasted_iota(jnp.int32, (rows, lanes), 0)

    def span_step(d, span_start):
        span_end = span_start + sl[d]
        overlap = (span_end > first) & (span_start < first + rows)

        def masked(s, row):
            return jnp.where((token >= span_start) & (token < span_end) & (token <= row), s, FLOOR)

        def chunk(n, carry):
            absorb(keys, values_t, n, jnp.maximum(span_start, first), span_end, masked)
            return carry

        low = own_chunk
        high = jnp.where(overlap, (span_end + rows - 1) // rows, low)
        lax.fori_loop(low, high, chunk, 0)
        return span_end

    lax.fori_loop(0, ndoc, span_step, jnp.int32(0))

    part_ref[...] = acc[...].astype(jnp.bfloat16)


def reduce_kernel(
    sizes, part_ref, stat_ref, out_ref,
    cr, cr_stat, sb, sb_stat, rb, rb_stat, fb, fb_stat, xr, xr_stat,
    core_send, core_recv, core_stat_send, core_stat_recv,
    ring_send, ring_recv, ring_stat_send, ring_stat_recv,
    x_send, x_recv, x_stat_send, x_stat_recv, out_send, out_recv, own_sem,
):
    at = Place(*sizes)
    Y, Z = at.Y, at.Z
    rows = out_ref.shape[0]
    others = [at.dev(x=(at.x + dx) % X) for dx in range(1, X)]
    plus, minus = at.along_z(1), at.along_z(-1)
    other_core = at.dev(c=1 - at.c)
    ends = [
        at.dev(y=(at.y + dy) % Y, c=(at.c + dc) % 2)
        for dc in range(2)
        for dy in range(Y)
        if dy or dc
    ]
    greet = others + ends + [plus]
    if Z > 2:
        greet.append(minus)
    barrier(greet)

    hops = ring_hops(Z)

    def slab_offset(direction, step):
        return Z // 2 - step if direction == 0 else -(Z // 2 - 1 - step)

    offsets = [slab_offset(*hop) for hop in hops] + [0]
    sent = []
    for i, offset in enumerate(offsets):
        z = at.z_at(-offset)
        a = remote(
            stat_ref.at[1 - at.c, z], cr_stat.at[z], core_stat_send.at[i], core_stat_recv.at[i],
            other_core,
        )
        b = remote(part_ref.at[1 - at.c, z], cr.at[z], core_send.at[i], core_recv.at[i], other_core)
        a.start()
        b.start()
        sent += [a, b]

    def from_core(i, offset):
        z = at.z_at(offset)
        remote(
            stat_ref.at[at.c, z], cr_stat.at[z], core_stat_send.at[i], core_stat_recv.at[i], other_core
        ).wait_recv()
        remote(
            part_ref.at[at.c, z], cr.at[z], core_send.at[i], core_recv.at[i], other_core
        ).wait_recv()
        return [(part_ref.at[at.c, z], stat_ref.at[at.c, z]), (cr.at[z], cr_stat.at[z])]

    def ring_in(direction, step, x):
        if x is None:
            remote(
                sb_stat.at[direction, step], rb_stat.at[direction, step],
                ring_stat_send.at[direction, step], ring_stat_recv.at[direction, step], plus,
            ).wait_recv()
        else:
            remote(
                sb.at[direction, step, x], rb.at[direction, step, x],
                ring_send.at[direction, step, x], ring_recv.at[direction, step, x], plus,
            ).wait_recv()

    def join(sources, came, to, to_stat, emit_stat, emit):
        for direction, step in came:
            ring_in(direction, step, None)
            sources = sources + [(rb.at[direction, step], rb_stat.at[direction, step])]
        stats = [stat[...] for _, stat in sources]
        top = functools.reduce(jnp.maximum, [s[:X] for s in stats])
        factors = [jnp.exp2(s[:X] - top) for s in stats]
        to_stat[:X, :] = top
        to_stat[X:, :] = sum(s[X:] * f for s, f in zip(stats, factors))
        emit_stat()
        for x in range(X):
            for direction, step in came:
                ring_in(direction, step, x)
            to[x] = sum(
                part[x].astype(jnp.float32) * f[x : x + 1] for (part, _), f in zip(sources, factors)
            ).astype(jnp.bfloat16)
            emit(x)

    for i, (direction, step) in enumerate(hops):
        device = plus if direction == 0 else minus

        def emit_stat():
            copy = remote(
                sb_stat.at[direction, step], rb_stat.at[direction, step],
                ring_stat_send.at[direction, step], ring_stat_recv.at[direction, step], device,
            )
            copy.start()
            sent.append(copy)

        def emit(x):
            copy = remote(
                sb.at[direction, step, x], rb.at[direction, step, x],
                ring_send.at[direction, step, x], ring_recv.at[direction, step, x], device,
            )
            copy.start()
            sent.append(copy)

        join(
            from_core(i, slab_offset(direction, step)),
            [(direction, step - 1)] if step else [],
            sb.at[direction, step], sb_stat.at[direction, step], emit_stat, emit,
        )

    came = [(0, Z // 2 - 1)] + ([(1, Z // 2 - 2)] if Z > 2 else [])
    join(from_core(Z - 1, 0), came, fb, fb_stat, lambda: None, lambda x: None)
    x_copies = []
    for dx in range(1, X):
        x = (at.x + dx) % X
        a = remote(fb_stat, xr_stat.at[at.x], x_stat_send.at[dx], x_stat_recv.at[dx], others[dx - 1])
        b = remote(fb.at[x], xr.at[at.x], x_send.at[dx], x_recv.at[dx], others[dx - 1])
        a.start()
        b.start()
        sent += [a, b]
        x_copies += [a, b]
    own = [
        pltpu.make_async_copy(fb.at[at.x], xr.at[at.x], own_sem.at[0]),
        pltpu.make_async_copy(fb_stat, xr_stat.at[at.x], own_sem.at[1]),
    ]
    for copy in own:
        copy.start()
    for copy in own:
        copy.wait()
    for copy in x_copies:
        copy.wait_recv()

    outs = []
    for hb, (one, two) in enumerate(((0, 3), (1, 2))):
        tops = [xr_stat[n, pl.ds(at.x, 1), :] for n in (one, two)]
        totals = [xr_stat[n, pl.ds(X + at.x, 1), :] for n in (one, two)]
        top = jnp.maximum(*tops)
        factors = [jnp.exp2(t - top) for t in tops]
        total = totals[0] * factors[0] + totals[1] * factors[1]
        value = xr[one].astype(jnp.float32) * factors[0] + xr[two].astype(jnp.float32) * factors[1]
        value = (value / total).T.astype(jnp.bfloat16)
        for h in range(2):
            column = pl.multiple_of((2 * at.y + hb) * (GROUP * HD) + at.c * (2 * HD) + h * HD, HD)
            out_ref[:, pl.ds(column, HD)] = value[h * rows : (h + 1) * rows]
        column = pl.multiple_of((2 * at.y + hb) * (GROUP * HD) + at.c * (2 * HD), 2 * HD)
        part = out_ref.at[:, pl.ds(column, 2 * HD)]
        for i, device in enumerate(ends):
            copy = remote(part, part, out_send.at[hb, i], out_recv.at[hb, i], device)
            copy.start()
            sent.append(copy)
    for hb in range(2):
        i = 0
        for dc in range(2):
            for dy in range(Y):
                if dy or dc:
                    y, c = (at.y - dy + Y) % Y, (at.c - dc + 2) % 2
                    column = pl.multiple_of((2 * y + hb) * (GROUP * HD) + c * (2 * HD), 2 * HD)
                    part = out_ref.at[:, pl.ds(column, 2 * HD)]
                    remote(part, part, out_send.at[hb, i], out_recv.at[hb, i], other_core).wait_recv()
                    i += 1
    for copy in sent:
        copy.wait_send()


def body(queries, span_keys, span_values, cache_keys, cache_values, cache_lengths, span_lengths):
    sizes = (lax.axis_size("ctx"), lax.axis_size("head"))
    Y, Z = sizes[0] // 2, sizes[1] // X
    heads = 2 * Y
    rows, tokens = queries.shape[0], cache_keys.shape[0]
    bf16, f32 = jnp.bfloat16, jnp.float32
    smem = pl.BlockSpec(memory_space=pltpu.SMEM)
    vmem = pl.BlockSpec(memory_space=pltpu.VMEM)
    hbm = pl.BlockSpec(memory_space=pl.ANY)
    dma = pltpu.SemaphoreType.DMA
    freq = jnp.asarray(inverse_freq())
    half = Z // 2

    q_all, k_all, v_all, sk, sv = pl.pallas_call(
        functools.partial(gather_kernel, sizes),
        out_shape=(
            jax.ShapeDtypeStruct((2, Z, X, 2 * rows, HD), bf16),
            jax.ShapeDtypeStruct((heads, tokens, HD), bf16),
            jax.ShapeDtypeStruct((heads, tokens, HD), bf16),
            jax.ShapeDtypeStruct((2, rows, HD), bf16),
            jax.ShapeDtypeStruct((2, rows, HD), bf16),
        ),
        in_specs=[smem, smem, vmem, hbm, hbm, hbm, vmem, hbm],
        out_specs=(vmem,) * 5,
        scratch_shapes=[
            VMEM((2, rows, 2 * HD), bf16),
            VMEM((2, rows, HD), bf16),
            VMEM((2, 2 * rows, HD), bf16),
            VMEM((rows, HD), bf16),
            VMEM((heads - 1, tokens, HD), bf16),
            dma((2,)), dma((3,)), dma((heads,)), dma((heads,)), dma((heads,)), dma((heads,)),
            dma((X,)), dma((X,)), dma((2, half, X)), dma((2, half, X)), dma((Z,)), dma((Z,)),
            dma((2,)), dma((2,)), dma((2,)),
        ],
        compiler_params=pltpu.CompilerParams(
            collective_id=0, has_side_effects=True, vmem_limit_bytes=40 * 1024 * 1024
        ),
        name="gather",
    )(cache_lengths, span_lengths, freq, queries, span_keys, span_values, cache_keys, cache_values)

    parts, stats = pl.pallas_call(
        functools.partial(attend_kernel, sizes),
        out_shape=(
            jax.ShapeDtypeStruct((2, Z, X, HD, 2 * rows), bf16),
            jax.ShapeDtypeStruct((2, Z, 2 * X, 2 * rows), f32),
        ),
        in_specs=[smem, smem] + [vmem] * 5,
        out_specs=(vmem, vmem),
        scratch_shapes=[VMEM((2, Z, X, HD, 2 * rows), f32)],
        compiler_params=pltpu.CompilerParams(vmem_limit_bytes=40 * 1024 * 1024),
        name="attend",
    )(cache_lengths, span_lengths, q_all, k_all, v_all, sk, sv)

    piece, stat = (HD, 2 * rows), (2 * X, 2 * rows)
    return pl.pallas_call(
        functools.partial(reduce_kernel, sizes),
        out_shape=jax.ShapeDtypeStruct(queries.shape, bf16),
        in_specs=[vmem, vmem],
        out_specs=vmem,
        scratch_shapes=[
            VMEM((Z, X) + piece, bf16), VMEM((Z,) + stat, f32),
            VMEM((2, half, X) + piece, bf16), VMEM((2, half) + stat, f32),
            VMEM((2, half, X) + piece, bf16), VMEM((2, half) + stat, f32),
            VMEM((X,) + piece, bf16), VMEM(stat, f32),
            VMEM((X,) + piece, bf16), VMEM((X,) + stat, f32),
            dma((Z,)), dma((Z,)), dma((Z,)), dma((Z,)),
            dma((2, half, X)), dma((2, half, X)), dma((2, half)), dma((2, half)),
            dma((X,)), dma((X,)), dma((X,)), dma((X,)),
            dma((2, 2 * Y)), dma((2, 2 * Y)), dma((2,)),
        ],
        compiler_params=pltpu.CompilerParams(
            collective_id=1, has_side_effects=True, vmem_limit_bytes=40 * 1024 * 1024
        ),
        name="reduce",
    )(parts, stats)


def solution(mesh):
    placed = (
        P("head", None),
        P("head", None),
        P("head", None),
        P(("ctx", "head"), None),
        P(("ctx", "head"), None),
        P(),
        P(),
    )
    return jax.shard_map(
        body, mesh=mesh, in_specs=placed, out_specs=P("head", None), check_vma=False
    )
```

time: 400 us -> 95.5 us (0.24)
  waiting for transfers between devices: 121 us -> 0 us
  Pallas kernels: 0 us -> 87.5 us
  matrix products: 70.8 us -> 0 us
  other arithmetic: 60.8 us -> 0 us
  blocking collectives: 51.4 us -> 0 us
  starting transfers between devices: 40.8 us -> 0 us
  local copies, waits for them, and re-layouts: 30.2 us -> 7.69 us
  between operations: 13.8 us -> 0.03 us
  loops' own time: 7.8 us -> 0 us
    all_to_all x5 -> x0, waiting for transfers between devices: 121 us -> none  [the longest x1 49.2 us: body(): lax.all_to_all(spread(turned_cache), 'head', split_axis=0, concat_axis=1,...]
    pallas_call x0 -> x3, Pallas kernels: none -> 87.5 us  [the longest x1 37.3 us: body(): pl.pallas_call(functools.partial(gather_kernel, sizes), out_shape=(jax.Sh...]
    dot_general x10 -> x0, matrix products: 70.8 us -> none  [the longest x5 44.2 us: absorb(): jnp.einsum('kgrn,knd->kgrd', weights.astype(jnp.bfloat16), value_block, p...]
    all_to_all x5 -> x0, starting transfers between devices: 40.7 us -> none  [the longest x1 11.9 us: body(): lax.all_to_all(turned_queries.transpose(1, 0, 2), 'head', split_axis=0, c...]
    reduce_sum x11 -> x0, other arithmetic: 36.4 us -> none  [the longest x5 35.2 us: absorb(): run_total = run_total * factor + jnp.sum(weights, axis=-1)]
    all_gather x2 -> x0, blocking collectives: 27.5 us -> none  [combined_all(): pieces = jax.tree.map(lambda part: lax.all_gather(part, axis), value)]
    all_to_all x1 -> x0, blocking collectives: 24 us -> none  [body(): lax.all_to_all(leaving, 'head', split_axis=0, concat_axis=1, tiled=True)]
    add x22 -> x0, other arithmetic: 15.2 us -> none  [the longest x7 14.6 us: combine(): left_sum * left_factor[..., None] + right_sum * right_factor[..., None]]
  transfers between devices with their start and end apart: 6 -> 0, of which waited for: 4 -> 0; matrix products, arithmetic and copies ran while one was open for 10% -> 0% of each run, Pallas kernels for 0% -> 0%
where the time goes in v1:
time: 95.5 us; the launch traced here: 95.2 us
  Pallas kernels  87.5 us (92%)
  local copies, waits for them, and re-layouts  7.69 us (8%)
    pallas_call x1, Pallas kernels, body(): pl.pallas_call(functools.partial(gather_kernel, sizes), out_shape=(jax.Sh...  37.3 us
    pallas_call x1, Pallas kernels, body(): pl.pallas_call(functools.partial(reduce_kernel, sizes), out_shape=jax.Sha...  31.8 us
    pallas_call x1, Pallas kernels, body(): pl.pallas_call(functools.partial(attend_kernel, sizes), out_shape=(jax.Sh...  18.4 us
    unnamed x17, local copies, waits for them, and re-layouts  7.69 us

profile of v1, /device:TPU:1, one launch (start us, length us, event | category | flops | bytes accessed | tf_op | source)
XLA Modules:
  0.0 95.2 jit_solution(9813632167681105280)
XLA Ops:
  0.0 0.0 copy-start
  0.0 1.0 %copy-done = bf16[64,4096]{1,0:T(8,128)(2,1)S(1)} copy-done((bf16[64,4096]{1,0:T(8,128)(2,1)S(1)}, bf16[64,4096]{1,0:T(8,128)(2,1)}, u32[]{:S(2)}) %copy-start) | copy-done | bytes 524312
  1.0 0.0 copy-start.1
  1.0 1.0 %copy-done.1 = bf16[256,1024]{1,0:T(8,128)(2,1)S(1)} copy-done((bf16[256,1024]{1,0:T(8,128)(2,1)S(1)}, bf16[256,1024]{1,0:T(8,128)(2,1)}, u32[]{:S(2)}) %copy-start.1) | copy-done | bytes 524312
  2.1 0.0 copy-start.2
  2.1 1.0 %copy-done.2 = bf16[256,1024]{1,0:T(8,128)(2,1)S(1)} copy-done((bf16[256,1024]{1,0:T(8,128)(2,1)S(1)}, bf16[256,1024]{1,0:T(8,128)(2,1)}, u32[]{:S(2)}) %copy-start.2) | copy-done | bytes 524312
  3.1 0.0 copy-start.3
  3.1 0.9 copy-done.3
  4.0 0.0 copy-start.4
  4.0 0.9 copy-done.4
  4.9 0.0 copy-start.5
  4.9 0.7 copy-done.5
  5.6 0.0 copy-start.6
  5.6 0.7 copy-done.6
  6.2 0.0 copy-start.7
  6.2 0.7 copy-done.7
  6.9 37.3 %gather.1 = (bf16[2,8,4,128,128]{4,3,2,1,0:T(8,128)(2,1)S(1)}, bf16[8,256,128]{2,1,0:T(8,128)(2,1)S(1)}, bf16[8,256,128]{2,1,0:T(8,128)(2,1)S(1)}, bf16[2,64,128...) custom-call(s32[16]{0:T(128)S(1)} %copy-done.5, s32[16]{0:T(128)S(1)} %copy-done.6, f32[1,128]{1,0:T(1,128)S(1)} %copy-done.7, ...), custom_call_target="tpu_custom_call" | custom-call | tf_op jit(solution)/shard_map/gather/pallas_call | solution.py:545
  44.2 18.4 %attend.1 = (bf16[2,8,4,128,128]{4,3,2,1,0:T(8,128)(2,1)S(1)}, f32[2,8,8,128]{3,2,1,0:T(8,128)S(1)}) custom-call(s32[16]{0:T(128)S(1)} %copy-done.5, s32[16]{0:T(128)S(1)} %copy-done.6, bf16[2,8,4,128,128]{4,3,2,1,0:T(8,128)(2,1)S(1)} %get-tuple-element.12.q_ref, bf16[8,256,128]{2,1,0:T(8,128)(2,1)S(1)} %get-tuple-element.13.k_ref, ...), custom_call_target="tpu_custom_call" | custom-call | tf_op jit(solution)/shard_map/attend/pallas_call | solution.py:572
  62.7 31.8 %reduce.1 = bf16[64,4096]{1,0:T(8,128)(2,1)S(1)} custom-call(bf16[2,8,4,128,128]{4,3,2,1,0:T(8,128)(2,1)S(1)} %get-tuple-element.17.part_ref, f32[2,8,8,128]{3,2,1,0:T(8,128)S(1)} %get-tuple-element.18.stat_ref), custom_call_target="tpu_custom_call" | custom-call | tf_op jit(solution)/shard_map/reduce/pallas_call | solution.py:586
  94.4 0.8 copy.10
Async XLA Ops:
  0.0 1.0 %copy-start = (bf16[64,4096]{1,0:T(8,128)(2,1)S(1)}, bf16[64,4096]{1,0:T(8,128)(2,1)}, u32[]{:S(2)}) copy-start(bf16[64,4096]{1,0:T(8,128)(2,1)} %q_ref.1) | copy-start | bytes 1572868
  1.0 1.0 %copy-start.1 = (bf16[256,1024]{1,0:T(8,128)(2,1)S(1)}, bf16[256,1024]{1,0:T(8,128)(2,1)}, u32[]{:S(2)}) copy-start(bf16[256,1024]{1,0:T(8,128)(2,1)} %k_ref.1) | copy-start | bytes 1572868
  2.1 1.0 %copy-start.2 = (bf16[256,1024]{1,0:T(8,128)(2,1)S(1)}, bf16[256,1024]{1,0:T(8,128)(2,1)}, u32[]{:S(2)}) copy-start(bf16[256,1024]{1,0:T(8,128)(2,1)} %v_ref.1) | copy-start | bytes 1572868
  3.1 0.9 copy-start.3
  4.0 0.9 copy-start.4
  4.9 0.7 copy-start.5
  5.6 0.7 copy-start.6
  6.2 0.7 copy-start.7

commit v2 on v1

--- a/solution.py
+++ b/solution.py
@@ -104,9 +104,9 @@
 
 
 def gather_kernel(
-    sizes, cl, sl, freq_ref, q_ref, sk_ref, sv_ref, k_ref, v_ref,
+    sizes, cl_ref, sl_ref, freq_ref, q_ref, sk_ref, sv_ref, k_ref, v_ref,
     qo, ko, vo, sko, svo,
-    q_in, sk_in, qs, sks, ks,
+    cl, sl, freq_in, k_in, q_in, sk_in, qs, sks, ks, in_sem,
     q_in_sem, span_sem, v_send, v_recv, k_send, k_recv, x_send, x_recv, ring_send, ring_recv,
     core_send, core_recv, own_sem, pair_send, pair_recv,
 ):
@@ -116,7 +116,12 @@
     rows, tokens = q_ref.shape[0], k_ref.shape[0]
     ndoc = cl.shape[0]
 
-    reads = []
+    reads = [
+        pltpu.make_async_copy(cl_ref, cl, in_sem.at[0]),
+        pltpu.make_async_copy(sl_ref, sl, in_sem.at[1]),
+        pltpu.make_async_copy(freq_ref, freq_in, in_sem.at[2]),
+    ]
+    k_read = pltpu.make_async_copy(k_ref, k_in, in_sem.at[3])
     for hb in range(2):
         column = pl.multiple_of((2 * at.y + hb) * (GROUP * HD) + at.c * (2 * HD), 2 * HD)
         reads.append(
@@ -130,6 +135,7 @@
         )
     for copy in reads:
         copy.start()
+    k_read.start()
     sv_copy = pltpu.make_async_copy(sv_ref.at[:, pl.ds(own, HD)], svo.at[0], span_sem.at[2])
     sv_copy.start()
     v_own = pltpu.make_async_copy(v_ref.at[:, pl.ds(own, HD)], vo.at[at.k], own_sem.at[0])
@@ -156,7 +162,9 @@
         copy.start()
         v_copies.append(copy)
 
-    freq = freq_ref[...]
+    for copy in reads:
+        copy.wait()
+    freq = freq_in[...]
     row = at.head * rows + lax.broadcasted_iota(jnp.int32, (rows, HD), 0)
     shift = jnp.zeros((rows, HD), jnp.int32)
     start = jnp.int32(0)
@@ -164,8 +172,6 @@
         shift = jnp.where(row >= start, cl[d] - start, shift)
         start = start + sl[d]
     cosine, sine = trig(row + shift, freq)
-    for copy in reads:
-        copy.wait()
     for hb in range(2):
         for h in range(2):
             qs[hb, h * rows : (h + 1) * rows, :] = turn(
@@ -235,27 +241,31 @@
         first = jnp.where(token >= start, start, first)
         start = start + cl[d]
     cosine, sine = trig(token - first, freq)
+    k_read.wait()
     k_copies = []
     for d in order:
         k, device = partners[d - 1]
         column = pl.multiple_of(k * HD, HD)
-        ks[d - 1] = turn(k_ref[:, pl.ds(column, HD)], cosine, sine)
+        ks[d - 1] = turn(k_in[:, pl.ds(column, HD)], cosine, sine)
         copy = remote(ks.at[d - 1], ko.at[at.k], k_send.at[d], k_recv.at[d], device)
         copy.start()
         k_copies.append(copy)
-    ko[at.k] = turn(k_ref[:, pl.ds(own, HD)], cosine, sine)
-
-    for i, (direction, step) in enumerate(hops):
-        onward = (direction, step + 1) in hops
+    ko[at.k] = turn(k_in[:, pl.ds(own, HD)], cosine, sine)
+
+    for step in range(Z // 2):
+        both = [direction for direction in range(2) if (direction, step) in hops]
         for n in range(X):
-            arrived(direction, step, n)
-            if onward:
-                copy = ring_copy(direction, step + 1, n)
-                copy.start()
-                ring.append(copy)
-        copy = core_copy(i + 1, -(step + 1) if direction == 0 else step + 1)
-        copy.start()
-        cores.append(copy)
+            for direction in both:
+                arrived(direction, step, n)
+                if (direction, step + 1) in hops:
+                    copy = ring_copy(direction, step + 1, n)
+                    copy.start()
+                    ring.append(copy)
+        for direction in both:
+            i = hops.index((direction, step))
+            copy = core_copy(i + 1, -(step + 1) if direction == 0 else step + 1)
+            copy.start()
+            cores.append(copy)
 
     for i in range(Z):
         if i == 0:
@@ -273,111 +283,178 @@
     sv_copy.wait()
 
 
-def attend_kernel(sizes, cl, sl, q_ref, k_ref, v_ref, sk_ref, sv_ref, part_ref, stat_ref, acc):
+def attend_kernel(
+    sizes, cl_ref, sl_ref, q_hbm, k_hbm, v_hbm, sk_hbm, sv_hbm, part_ref, stat_ref,
+    acc, cl, sl, q_ref, k_ref, v_ref, vt_ref, s_even, s_odd, w_odd, f_odd,
+    cache_at, span_at, g_block, g_low, g_high, g_first, g_end, g_causal, e_group, e_chunk, in_sem,
+):
     at = Place(*sizes)
     Z = at.Z
-    blocks, tokens, _ = k_ref.shape
-    rows = q_ref.shape[3] // 2
+    blocks, tokens, _ = k_hbm.shape
+    rows = sk_hbm.shape[1]
     lanes = 4 * rows
     ndoc = cl.shape[0]
-
+    pairs = (
+        (cl_ref, cl), (sl_ref, sl), (k_hbm, k_ref.at[pl.ds(0, blocks)]),
+        (q_hbm, q_ref), (v_hbm, v_ref.at[pl.ds(0, blocks)]),
+        (sk_hbm.at[at.c], k_ref.at[blocks, pl.ds(0, rows)]),
+        (sv_hbm.at[at.c], v_ref.at[blocks, pl.ds(0, rows)]),
+    )
+    reads = [pltpu.make_async_copy(a, b, in_sem.at[i]) for i, (a, b) in enumerate(pairs)]
+    for copy in reads:
+        copy.start()
+
+    k_ref[blocks, rows:, :] = jnp.zeros((tokens - rows, HD), jnp.bfloat16)
+    v_ref[blocks, rows:, :] = jnp.zeros((tokens - rows, HD), jnp.bfloat16)
     half = lax.broadcasted_iota(jnp.int32, (2, Z, 2 * X, 2 * rows), 2)
     stat_ref[...] = jnp.where(half < X, FLOOR, 0.0)
     acc[...] = jnp.zeros_like(acc)
+    w_odd[...] = jnp.zeros_like(w_odd)
+    f_odd[...] = jnp.ones_like(f_odd)
+    reads[0].wait()
+    reads[1].wait()
+
+    cache_at[0] = jnp.int32(0)
+    span_at[0] = jnp.int32(0)
+    for d in range(ndoc):
+        cache_at[d + 1] = cache_at[d] + cl[d]
+        span_at[d + 1] = span_at[d] + sl[d]
+
+    far = jnp.int32(1 << 20)
+
+    def none(group):
+        g_block[group], g_low[group], g_high[group] = jnp.int32(0), jnp.int32(0), jnp.int32(0)
+        g_first[group], g_end[group], g_causal[group] = jnp.int32(0), jnp.int32(0), far
+
+    none(0)
+    e_group[0], e_chunk[0] = jnp.int32(0), jnp.int32(0)
+
+    def add_block(counts, block, starts, first, width, causal, row_first):
+        doc_first, doc_last = jnp.int32(0), jnp.int32(0)
+        for d in range(1, ndoc):
+            doc_first += (starts[d] <= first).astype(jnp.int32)
+            doc_last += (starts[d] < first + width).astype(jnp.int32)
+
+        def add_doc(d, counts):
+            group, entry = counts
+            g_block[group] = block
+            g_low[group] = jnp.maximum(starts[d] - first, 0)
+            g_high[group] = jnp.minimum(starts[d + 1] - first, width)
+            g_first[group] = jnp.maximum(span_at[d], row_first)
+            g_end[group] = span_at[d + 1]
+            g_causal[group] = causal
+            low = jnp.maximum(span_at[d], row_first) // rows
+            high = (span_at[d + 1] + rows - 1) // rows
+
+            def add_chunk(n, entry):
+                e_group[entry] = group
+                e_chunk[entry] = n
+                return entry + 1
+
+            return group + 1, lax.fori_loop(low, high, add_chunk, entry)
+
+        return lax.fori_loop(doc_first, doc_last + 1, add_doc, counts)
+
+    def cache_block(b, counts):
+        x = at.pair * 3 + (b % 2) * (1 - 2 * at.pair)
+        first = (((b // 2) * 2 + at.c) * sizes[1] + x * Z + at.z) * tokens
+        return add_block(counts, b, cache_at, first, tokens, far, 0)
+
+    counts = lax.fori_loop(0, blocks, cache_block, (jnp.int32(1), jnp.int32(1)))
+    mate = at.pair * 3 + (1 - at.hb) * (1 - 2 * at.pair)
+    first = (jnp.where(at.c == 0, at.x, mate) * Z + at.z) * rows
+    _, count = add_block(counts, jnp.int32(blocks), span_at, first, rows, -first, first)
+    for i in range(4):
+        e_group[count + i], e_chunk[count + i] = jnp.int32(0), jnp.int32(0)
+
+    for copy in reads[2:]:
+        copy.wait()
+
+    def turn_over(b, carry):
+        vt_ref[b] = v_ref[b].T
+        return carry
+
+    lax.fori_loop(0, blocks + 1, turn_over, 0)
+
     lane = lax.broadcasted_iota(jnp.int32, (1, lanes), 1) % rows
-
-    def absorb(keys, values_t, n, row_low, row_high, masked):
+    token = lax.broadcasted_iota(jnp.int32, (tokens, lanes), 0)
+
+    def scores(i):
+        n = e_chunk[i]
         x, z = n // Z, n % Z
         q = jnp.concatenate([q_ref[0, z, x], q_ref[1, z, x]], axis=0)
-        s = lax.dot_general(
-            keys, q, (((1,), (1,)), ((), ())), preferred_element_type=jnp.float32
+        return lax.dot_general(
+            k_ref[g_block[e_group[i]]], q, (((1,), (1,)), ((), ())),
+            preferred_element_type=jnp.float32,
         )
+
+    def soften(i, s):
+        group, n = e_group[i], e_chunk[i]
+        x, z = n // Z, n % Z
         row = n * rows + lane
-        s = masked(s * SCALE, row)
-        m_old = jnp.concatenate(
-            [stat_ref[0, z, pl.ds(x, 1), :], stat_ref[1, z, pl.ds(x, 1), :]], axis=1
-        )
-        l_old = jnp.concatenate(
-            [stat_ref[0, z, pl.ds(X + x, 1), :], stat_ref[1, z, pl.ds(X + x, 1), :]], axis=1
-        )
-        here = (row >= row_low) & (row < row_high)
+        here = (row >= g_first[group]) & (row < g_end[group])
+        high = jnp.minimum(g_high[group], row + g_causal[group] + 1)
+        s = jnp.where((token >= g_low[group]) & (token < high), s * SCALE, FLOOR)
+        m_old = jnp.concatenate([stat_ref[c, z, pl.ds(x, 1), :] for c in range(2)], axis=1)
+        l_old = jnp.concatenate([stat_ref[c, z, pl.ds(X + x, 1), :] for c in range(2)], axis=1)
         m_new = jnp.where(here, jnp.maximum(m_old, jnp.max(s, axis=0, keepdims=True)), m_old)
         w = jnp.exp2(s - jnp.where(here, m_new, -FLOOR))
         factor = jnp.exp2(m_old - m_new)
         l_new = l_old * factor + jnp.sum(w, axis=0, keepdims=True)
-        o = jnp.dot(values_t, w.astype(jnp.bfloat16), preferred_element_type=jnp.float32)
         for c in range(2):
             part = slice(c * 2 * rows, (c + 1) * 2 * rows)
             stat_ref[c, z, pl.ds(x, 1), :] = m_new[:, part]
             stat_ref[c, z, pl.ds(X + x, 1), :] = l_new[:, part]
+        return w.astype(jnp.bfloat16), factor
+
+    def product(i, w):
+        return jnp.dot(vt_ref[g_block[e_group[i]]], w, preferred_element_type=jnp.float32)
+
+    def update(i, o, factor):
+        n = e_chunk[i]
+        x, z = n // Z, n % Z
+        for c in range(2):
+            part = slice(c * 2 * rows, (c + 1) * 2 * rows)
             acc[c, z, x] = acc[c, z, x] * factor[:, part] + o[:, part]
 
-    def block_step(b, carry):
-        first = (((b // 2) * 2 + at.c) * sizes[1] + (at.pair * 3 + (b % 2) * (1 - 2 * at.pair)) * Z + at.z) * tokens
-        keys = k_ref[b]
-        values_t = v_ref[b].T
-        token = first + lax.broadcasted_iota(jnp.int32, (tokens, lanes), 0)
-
-        def doc_step(d, carry):
-            cache_start, span_start = carry
-            cache_end, span_end = cache_start + cl[d], span_start + sl[d]
-            overlap = (cache_end > first) & (cache_start < first + tokens)
-
-            def masked(s, row):
-                return jnp.where((token >= cache_start) & (token < cache_end), s, FLOOR)
-
-            def chunk(n, carry):
-                absorb(keys, values_t, n, span_start, span_end, masked)
-                return carry
-
-            low = span_start // rows
-            high = jnp.where(overlap, (span_end + rows - 1) // rows, low)
-            lax.fori_loop(low, high, chunk, 0)
-            return cache_end, span_end
-
-        lax.fori_loop(0, ndoc, doc_step, (jnp.int32(0), jnp.int32(0)))
+    s_even[...] = scores(1)
+
+    def step(j, carry):
+        i = 2 * j + 1
+        s_odd[...] = scores(i + 1)
+        o_before = product(i - 1, w_odd[...])
+        w, factor = soften(i, s_even[...])
+        update(i - 1, o_before, f_odd[...])
+        s_even[...] = scores(i + 2)
+        o = product(i, w)
+        w_next, factor_next = soften(i + 1, s_odd[...])
+        update(i, o, factor)
+        w_odd[...] = w_next
+        f_odd[...] = factor_next
         return carry
 
-    lax.fori_loop(0, blocks, block_step, 0)
-
-    mate = at.pair * 3 + (1 - at.hb) * (1 - 2 * at.pair)
-    own_chunk = jnp.where(at.c == 0, at.x, mate) * Z + at.z
-    first = own_chunk * rows
-    keys = sk_ref[at.c]
-    values_t = sv_ref[at.c].T
-    token = first + lax.broadcasted_iota(jnp.int32, (rows, lanes), 0)
-
-    def span_step(d, span_start):
-        span_end = span_start + sl[d]
-        overlap = (span_end > first) & (span_start < first + rows)
-
-        def masked(s, row):
-            return jnp.where((token >= span_start) & (token < span_end) & (token <= row), s, FLOOR)
-
-        def chunk(n, carry):
-            absorb(keys, values_t, n, jnp.maximum(span_start, first), span_end, masked)
-            return carry
-
-        low = own_chunk
-        high = jnp.where(overlap, (span_end + rows - 1) // rows, low)
-        lax.fori_loop(low, high, chunk, 0)
-        return span_end
-
-    lax.fori_loop(0, ndoc, span_step, jnp.int32(0))
-
+    steps = count // 2
+    lax.fori_loop(0, steps, step, 0)
+    update(2 * steps, product(2 * steps, w_odd[...]), f_odd[...])
     part_ref[...] = acc[...].astype(jnp.bfloat16)
 
 
 def reduce_kernel(
-    sizes, part_ref, stat_ref, out_ref,
-    cr, cr_stat, sb, sb_stat, rb, rb_stat, fb, fb_stat, xr, xr_stat,
+    sizes, part_hbm, stat_hbm, out_ref,
+    part_ref, stat_ref, cr, cr_stat, sb, sb_stat, rb, rb_stat, fb, fb_stat, xr, xr_stat,
     core_send, core_recv, core_stat_send, core_stat_recv,
     ring_send, ring_recv, ring_stat_send, ring_stat_recv,
-    x_send, x_recv, x_stat_send, x_stat_recv, out_send, out_recv, own_sem,
+    x_send, x_recv, x_stat_send, x_stat_recv, out_send, out_recv, own_sem, in_sem,
 ):
     at = Place(*sizes)
     Y, Z = at.Y, at.Z
     rows = out_ref.shape[0]
+    reads = [
+        pltpu.make_async_copy(stat_hbm.at[at.c], stat_ref, in_sem.at[0]),
+        pltpu.make_async_copy(part_hbm.at[at.c], part_ref, in_sem.at[1]),
+    ]
+    for copy in reads:
+        copy.start()
     others = [at.dev(x=(at.x + dx) % X) for dx in range(1, X)]
     plus, minus = at.along_z(1), at.along_z(-1)
     other_core = at.dev(c=1 - at.c)
@@ -402,10 +479,10 @@
     for i, offset in enumerate(offsets):
         z = at.z_at(-offset)
         a = remote(
-            stat_ref.at[1 - at.c, z], cr_stat.at[z], core_stat_send.at[i], core_stat_recv.at[i],
+            stat_hbm.at[1 - at.c, z], cr_stat.at[z], core_stat_send.at[i], core_stat_recv.at[i],
             other_core,
         )
-        b = remote(part_ref.at[1 - at.c, z], cr.at[z], core_send.at[i], core_recv.at[i], other_core)
+        b = remote(part_hbm.at[1 - at.c, z], cr.at[z], core_send.at[i], core_recv.at[i], other_core)
         a.start()
         b.start()
         sent += [a, b]
@@ -413,12 +490,12 @@
     def from_core(i, offset):
         z = at.z_at(offset)
         remote(
-            stat_ref.at[at.c, z], cr_stat.at[z], core_stat_send.at[i], core_stat_recv.at[i], other_core
+            stat_ref.at[z], cr_stat.at[z], core_stat_send.at[i], core_stat_recv.at[i], other_core
         ).wait_recv()
         remote(
-            part_ref.at[at.c, z], cr.at[z], core_send.at[i], core_recv.at[i], other_core
+            part_ref.at[z], cr.at[z], core_send.at[i], core_recv.at[i], other_core
         ).wait_recv()
-        return [(part_ref.at[at.c, z], stat_ref.at[at.c, z]), (cr.at[z], cr_stat.at[z])]
+        return [(part_ref.at[z], stat_ref.at[z]), (cr.at[z], cr_stat.at[z])]
 
     def ring_in(direction, step, x):
         if x is None:
@@ -432,7 +509,7 @@
                 ring_send.at[direction, step, x], ring_recv.at[direction, step, x], plus,
             ).wait_recv()
 
-    def join(sources, came, to, to_stat, emit_stat, emit):
+    def join(sources, came, to, to_stat, emit):
         for direction, step in came:
             ring_in(direction, step, None)
             sources = sources + [(rb.at[direction, step], rb_stat.at[direction, step])]
@@ -441,8 +518,9 @@
         factors = [jnp.exp2(s[:X] - top) for s in stats]
         to_stat[:X, :] = top
         to_stat[X:, :] = sum(s[X:] * f for s, f in zip(stats, factors))
-        emit_stat()
-        for x in range(X):
+        emit(None)
+
+        def piece(x):
             for direction, step in came:
                 ring_in(direction, step, x)
             to[x] = sum(
@@ -450,42 +528,59 @@
             ).astype(jnp.bfloat16)
             emit(x)
 
-    for i, (direction, step) in enumerate(hops):
+        return piece
+
+    def ring_out(direction, step):
         device = plus if direction == 0 else minus
 
-        def emit_stat():
-            copy = remote(
-                sb_stat.at[direction, step], rb_stat.at[direction, step],
-                ring_stat_send.at[direction, step], ring_stat_recv.at[direction, step], device,
-            )
+        def emit(x):
+            if x is None:
+                copy = remote(
+                    sb_stat.at[direction, step], rb_stat.at[direction, step],
+                    ring_stat_send.at[direction, step], ring_stat_recv.at[direction, step], device,
+                )
+            else:
+                copy = remote(
+                    sb.at[direction, step, x], rb.at[direction, step, x],
+                    ring_send.at[direction, step, x], ring_recv.at[direction, step, x], device,
+                )
             copy.start()
             sent.append(copy)
 
-        def emit(x):
-            copy = remote(
-                sb.at[direction, step, x], rb.at[direction, step, x],
-                ring_send.at[direction, step, x], ring_recv.at[direction, step, x], device,
+        return emit
+
+    for copy in reads:
+        copy.wait()
+    for step in range(Z // 2):
+        pieces = [
+            join(
+                from_core(i, slab_offset(*hop)), [(hop[0], step - 1)] if step else [],
+                sb.at[hop[0], step], sb_stat.at[hop[0], step], ring_out(*hop),
             )
-            copy.start()
-            sent.append(copy)
-
-        join(
-            from_core(i, slab_offset(direction, step)),
-            [(direction, step - 1)] if step else [],
-            sb.at[direction, step], sb_stat.at[direction, step], emit_stat, emit,
-        )
+            for i, hop in enumerate(hops)
+            if hop[1] == step
+        ]
+        for x in range(X):
+            for piece in pieces:
+                piece(x)
 
     came = [(0, Z // 2 - 1)] + ([(1, Z // 2 - 2)] if Z > 2 else [])
-    join(from_core(Z - 1, 0), came, fb, fb_stat, lambda: None, lambda x: None)
+    piece = join(from_core(Z - 1, 0), came, fb, fb_stat, lambda x: None)
     x_copies = []
     for dx in range(1, X):
+        copy = remote(
+            fb_stat, xr_stat.at[at.x], x_stat_send.at[dx], x_stat_recv.at[dx], others[dx - 1]
+        )
+        copy.start()
+        x_copies.append(copy)
+    for x in range(X):
+        piece(x)
+    for dx in range(1, X):
         x = (at.x + dx) % X
-        a = remote(fb_stat, xr_stat.at[at.x], x_stat_send.at[dx], x_stat_recv.at[dx], others[dx - 1])
-        b = remote(fb.at[x], xr.at[at.x], x_send.at[dx], x_recv.at[dx], others[dx - 1])
-        a.start()
-        b.start()
-        sent += [a, b]
-        x_copies += [a, b]
+        copy = remote(fb.at[x], xr.at[at.x], x_send.at[dx], x_recv.at[dx], others[dx - 1])
+        copy.start()
+        x_copies.append(copy)
+    sent += x_copies
     own = [
         pltpu.make_async_copy(fb.at[at.x], xr.at[at.x], own_sem.at[0]),
         pltpu.make_async_copy(fb_stat, xr_stat.at[at.x], own_sem.at[1]),
@@ -535,9 +630,9 @@
     heads = 2 * Y
     rows, tokens = queries.shape[0], cache_keys.shape[0]
     bf16, f32 = jnp.bfloat16, jnp.float32
-    smem = pl.BlockSpec(memory_space=pltpu.SMEM)
+    lengths = pltpu.SMEM(cache_lengths.shape, jnp.int32)
     vmem = pl.BlockSpec(memory_space=pltpu.VMEM)
-    hbm = pl.BlockSpec(memory_space=pl.ANY)
+    hbm = pl.BlockSpec(memory_space=pltpu.HBM)
     dma = pltpu.SemaphoreType.DMA
     freq = jnp.asarray(inverse_freq())
     half = Z // 2
@@ -551,23 +646,31 @@
             jax.ShapeDtypeStruct((2, rows, HD), bf16),
             jax.ShapeDtypeStruct((2, rows, HD), bf16),
         ),
-        in_specs=[smem, smem, vmem, hbm, hbm, hbm, vmem, hbm],
+        in_specs=[hbm] * 8,
         out_specs=(vmem,) * 5,
         scratch_shapes=[
+            lengths, lengths, VMEM(freq.shape, f32), VMEM((tokens, heads * HD), bf16),
             VMEM((2, rows, 2 * HD), bf16),
             VMEM((2, rows, HD), bf16),
             VMEM((2, 2 * rows, HD), bf16),
             VMEM((rows, HD), bf16),
             VMEM((heads - 1, tokens, HD), bf16),
-            dma((2,)), dma((3,)), dma((heads,)), dma((heads,)), dma((heads,)), dma((heads,)),
+            dma((4,)), dma((2,)), dma((3,)), dma((heads,)), dma((heads,)), dma((heads,)), dma((heads,)),
             dma((X,)), dma((X,)), dma((2, half, X)), dma((2, half, X)), dma((Z,)), dma((Z,)),
             dma((2,)), dma((2,)), dma((2,)),
         ],
         compiler_params=pltpu.CompilerParams(
-            collective_id=0, has_side_effects=True, vmem_limit_bytes=40 * 1024 * 1024
+            collective_id=0, has_side_effects=True, vmem_limit_bytes=60 * 1024 * 1024
         ),
         name="gather",
     )(cache_lengths, span_lengths, freq, queries, span_keys, span_values, cache_keys, cache_values)
+
+    ndoc = cache_lengths.shape[0]
+    groups = (heads + 1) * ndoc + 1
+    entries = (heads + 1) * (X * Z + ndoc) + 8
+
+    def numbers(n):
+        return pltpu.SMEM((n,), jnp.int32)
 
     parts, stats = pl.pallas_call(
         functools.partial(attend_kernel, sizes),
@@ -575,10 +678,18 @@
             jax.ShapeDtypeStruct((2, Z, X, HD, 2 * rows), bf16),
             jax.ShapeDtypeStruct((2, Z, 2 * X, 2 * rows), f32),
         ),
-        in_specs=[smem, smem] + [vmem] * 5,
+        in_specs=[hbm] * 7,
         out_specs=(vmem, vmem),
-        scratch_shapes=[VMEM((2, Z, X, HD, 2 * rows), f32)],
-        compiler_params=pltpu.CompilerParams(vmem_limit_bytes=40 * 1024 * 1024),
+        scratch_shapes=[
+            VMEM((2, Z, X, HD, 2 * rows), f32), lengths, lengths, VMEM(q_all.shape, bf16),
+            VMEM((heads + 1, tokens, HD), bf16), VMEM((heads + 1, tokens, HD), bf16),
+            VMEM((heads + 1, HD, tokens), bf16),
+            VMEM((tokens, 4 * rows), f32), VMEM((tokens, 4 * rows), f32),
+            VMEM((tokens, 4 * rows), bf16), VMEM((1, 4 * rows), f32),
+            numbers(ndoc + 1), numbers(ndoc + 1), *[numbers(groups)] * 6,
+            numbers(entries), numbers(entries), dma((7,)),
+        ],
+        compiler_params=pltpu.CompilerParams(vmem_limit_bytes=60 * 1024 * 1024),
         name="attend",
     )(cache_lengths, span_lengths, q_all, k_all, v_all, sk, sv)
 
@@ -586,9 +697,10 @@
     return pl.pallas_call(
         functools.partial(reduce_kernel, sizes),
         out_shape=jax.ShapeDtypeStruct(queries.shape, bf16),
-        in_specs=[vmem, vmem],
+        in_specs=[hbm, hbm],
         out_specs=vmem,
         scratch_shapes=[
+            VMEM((Z, X) + piece, bf16), VMEM((Z,) + stat, f32),
             VMEM((Z, X) + piece, bf16), VMEM((Z,) + stat, f32),
             VMEM((2, half, X) + piece, bf16), VMEM((2, half) + stat, f32),
             VMEM((2, half, X) + piece, bf16), VMEM((2, half) + stat, f32),
@@ -597,10 +709,10 @@
             dma((Z,)), dma((Z,)), dma((Z,)), dma((Z,)),
             dma((2, half, X)), dma((2, half, X)), dma((2, half)), dma((2, half)),
             dma((X,)), dma((X,)), dma((X,)), dma((X,)),
-            dma((2, 2 * Y)), dma((2, 2 * Y)), dma((2,)),
+            dma((2, 2 * Y)), dma((2, 2 * Y)), dma((2,)), dma((2,)),
         ],
         compiler_params=pltpu.CompilerParams(
-            collective_id=1, has_side_effects=True, vmem_limit_bytes=40 * 1024 * 1024
+            collective_id=1, has_side_effects=True, vmem_limit_bytes=60 * 1024 * 1024
         ),
         name="reduce",
     )(parts, stats)

time: 95.5 us -> 80 us (0.84)
  Pallas kernels: 87.5 us -> 77.9 us
  local copies, waits for them, and re-layouts: 7.69 us -> 1.87 us
    pallas_call x1, Pallas kernels: 18.4 us -> 7.95 us  [body(): pl.pallas_call(functools.partial(attend_kernel, sizes), out_shape=(jax.Sh...]
    unnamed x17 -> x1, local copies, waits for them, and re-layouts: 7.69 us -> 1.87 us
    pallas_call x1, Pallas kernels: 37.3 us -> 38.5 us  [body(): pl.pallas_call(functools.partial(gather_kernel, sizes), out_shape=(jax.Sh...]
where the time goes in v2:
time: 80 us; the launch traced here: 79.8 us
  Pallas kernels  77.9 us (97%)
  local copies, waits for them, and re-layouts  1.87 us (2%)
    pallas_call x1, Pallas kernels, body(): pl.pallas_call(functools.partial(gather_kernel, sizes), out_shape=(jax.Sh...  38.5 us
    pallas_call x1, Pallas kernels, body(): pl.pallas_call(functools.partial(reduce_kernel, sizes), out_shape=jax.Sha...  31.5 us
    pallas_call x1, Pallas kernels, body(): pl.pallas_call(functools.partial(attend_kernel, sizes), out_shape=(jax.Sh...  7.95 us
    unnamed x1, local copies, waits for them, and re-layouts  1.87 us

profile of v2, /device:TPU:1, one launch (start us, length us, event | category | flops | bytes accessed | tf_op | source)
XLA Modules:
  0.0 79.8 jit_solution(17090566661038702920)
XLA Ops:
  0.0 38.5 %gather.1 = (bf16[2,8,4,128,128]{4,3,2,1,0:T(8,128)(2,1)}, bf16[8,256,128]{2,1,0:T(8,128)(2,1)}, bf16[8,256,128]{2,1,0:T(8,128)(2,1)}, bf16[2,64,128]{2,1,0:T(8,128)(2,1)}, bf16[2,64,128]{2,1,0:T(8,128)(2,1)}) custom-call(s32[16]{0:T(128)} %cl_ref.3, s32[16]{0:T(128)} %sl_ref.3, f32[1,128]{1,0:T(1,128)} %constant.2.clone.freq_ref, bf16[64,4096]{1,0:T(8,128)(2,1)} %q_ref.1, ...), custom_call_target="tpu_custom_call" | custom-call | tf_op jit(solution)/shard_map/gather/pallas_call | solution.py:640
  38.6 8.0 %attend.1 = (bf16[2,8,4,128,128]{4,3,2,1,0:T(8,128)(2,1)}, f32[2,8,8,128]{3,2,1,0:T(8,128)}) custom-call(s32[16]{0:T(128)} %cl_ref.3, s32[16]{0:T(128)} %sl_ref.3, bf16[2,8,4,128,128]{4,3,2,1,0:T(8,128)(2,1)} %get-tuple-element.12.q_hbm, bf16[8,256,128]{2,1,0:T(8,128)(2,1)} %get-tuple-element.13.k_hbm, bf16[8,256,128]{2,1,0:T(8,128)(2,1)} %get-tuple-element.14.v_hbm, ...), custom_call_target="tpu_custom_call" | custom-call | tf_op jit(solution)/shard_map/attend/pallas_call | solution.py:675
  46.5 31.5 %reduce.1 = bf16[64,4096]{1,0:T(8,128)(2,1)} custom-call(bf16[2,8,4,128,128]{4,3,2,1,0:T(8,128)(2,1)} %get-tuple-element.17.part_hbm, f32[2,8,8,128]{3,2,1,0:T(8,128)} %get-tuple-element.18.stat_hbm), custom_call_target="tpu_custom_call" | custom-call | tf_op jit(solution)/shard_map/reduce/pallas_call | solution.py:697
  78.0 1.9 %copy.10 = bf16[64,4096]{1,0:T(8,128)(2,1)} copy(bf16[64,4096]{1,0:T(8,128)(2,1)} %reduce.1) | data formatting | bytes 1048576

commit v3 on v2

--- a/solution.py
+++ b/solution.py
@@ -42,6 +42,7 @@
         self.pair = self.x // 2
         self.hb = self.bit_of(self.x)
         self.k = 2 * self.y + self.hb
+        self.mate = self.pair * 3 + (1 - self.hb) * (1 - 2 * self.pair)
         self.sgn = 1 - 2 * self.c
 
     def bit_of(self, x):
@@ -61,6 +62,14 @@
     def along_z(self, offset):
         return self.dev(z=self.z_at(offset))
 
+    def around(self):
+        return [
+            (dz, dx, self.dev(x=(self.x + dx) % X, z=self.z_at(dz)))
+            for dz in (1, -1, 0)
+            for dx in range(X)
+            if dz or dx
+        ]
+
     def key_partner(self, d):
         k = (self.k + d) % (2 * self.Y)
         hb = k % 2
@@ -93,21 +102,11 @@
     return jnp.cos(angle), jnp.where(lane < HD // 2, -sine, sine)
 
 
-def ring_hops(Z):
-    near, far = Z // 2 - 1, Z // 2
-    hops = []
-    for step in range(far):
-        hops.append((0, step))
-        if step < near:
-            hops.append((1, step))
-    return hops
-
-
 def gather_kernel(
     sizes, cl_ref, sl_ref, freq_ref, q_ref, sk_ref, sv_ref, k_ref, v_ref,
     qo, ko, vo, sko, svo,
     cl, sl, freq_in, k_in, q_in, sk_in, qs, sks, ks, in_sem,
-    q_in_sem, span_sem, v_send, v_recv, k_send, k_recv, x_send, x_recv, ring_send, ring_recv,
+    q_in_sem, span_sem, v_send, v_recv, k_send, k_recv, q_send, q_recv, on_send,
     core_send, core_recv, own_sem, pair_send, pair_recv,
 ):
     at = Place(*sizes)
@@ -142,13 +141,10 @@
     v_own.start()
 
     partners = [at.key_partner(d) for d in range(1, heads)]
-    others = [at.dev(x=(at.x + dx) % X) for dx in range(1, X)]
-    plus, minus = at.along_z(1), at.along_z(-1)
     other_core = at.dev(c=1 - at.c)
-    outside = [at.dev(x=(at.x + 2) % X), at.dev(x=3 - at.x)]
-    greet = [device for _, device in partners] + outside + [other_core, plus]
-    if Z > 2:
-        greet.append(minus)
+    around = at.around()
+    greet = [at.dev(y=(at.y + dy) % Y, x=x) for dy in range(1, Y) for x in (at.x, at.mate)]
+    greet += [device for _, _, device in around] + [at.along_z(2), at.along_z(-2), other_core]
     barrier(greet)
 
     order = sorted(range(1, heads), key=lambda d: -min(d, heads - d))
@@ -180,59 +176,52 @@
     sko[0] = turn(sk_in[0], cosine, sine)
     sks[...] = turn(sk_in[1], cosine, sine)
 
-    x_copies = []
-    for dx in range(1, X):
-        x = (at.x + dx) % X
+    q_own = pltpu.make_async_copy(qs.at[at.hb], qo.at[at.c, at.z, at.x], own_sem.at[1])
+    q_own.start()
+    first_copies = []
+    for dz, dx, device in around:
         copy = remote(
-            qs.at[at.bit_of(x)], qo.at[at.c, at.z, at.x], x_send.at[dx], x_recv.at[dx], others[dx - 1]
+            qs.at[at.bit_of((at.x + dx) % X)], qo.at[at.c, at.z, at.x],
+            q_send.at[dz + 1, dx], q_recv.at[-dz + 4, dx], device,
         )
         copy.start()
-        x_copies.append(copy)
-    mate = at.dev(x=at.pair * 3 + (1 - at.hb) * (1 - 2 * at.pair))
+        first_copies.append(copy)
     pair_copies = [
-        remote(sks, sko.at[1], pair_send.at[0], pair_recv.at[0], mate),
-        remote(sv_ref.at[:, pl.ds(theirs, HD)], svo.at[1], pair_send.at[1], pair_recv.at[1], mate),
+        remote(sks, sko.at[1], pair_send.at[0], pair_recv.at[0], at.dev(x=at.mate)),
+        remote(
+            sv_ref.at[:, pl.ds(theirs, HD)], svo.at[1], pair_send.at[1], pair_recv.at[1],
+            at.dev(x=at.mate),
+        ),
     ]
     for copy in pair_copies:
         copy.start()
-    q_own = pltpu.make_async_copy(qs.at[at.hb], qo.at[at.c, at.z, at.x], own_sem.at[1])
-    q_own.start()
-
-    def ring_copy(direction, step, n):
-        offset = -step if direction == 0 else step
-        x = (at.x - n + X) % X
-        part = qo.at[at.c, at.z_at(offset), x]
-        return remote(
-            part, part, ring_send.at[direction, step, n], ring_recv.at[direction, step, n],
-            plus if direction == 0 else minus,
+
+    onward = []
+
+    def piece(offset, n):
+        return qo.at[at.c, at.z_at(offset), (at.x - n + X) % X]
+
+    def arrived(offset, n):
+        part = piece(offset, n)
+        remote(part, part, q_send.at[0, 0], q_recv.at[offset + 4, n], other_core).wait_recv()
+
+    def pass_on(offset, n, far):
+        part = piece(offset, n)
+        copy = remote(
+            part, part, on_send.at[len(onward)], q_recv.at[offset - far + 4, n], at.along_z(far)
         )
-
-    def arrived(direction, step, n):
-        offset = -(step + 1) if direction == 0 else step + 1
-        x = (at.x - n + X) % X
-        part = qo.at[at.c, at.z_at(offset), x]
-        remote(
-            part, part, ring_send.at[direction, step, n], ring_recv.at[direction, step, n], plus
-        ).wait_recv()
-
-    def core_copy(i, offset):
+        copy.start()
+        onward.append(copy)
+
+    slabs = (0, -1, 1, -2, 2, -3, 3, -4)
+    cores = []
+
+    def to_core(offset):
+        i = slabs.index(offset)
         slab = qo.at[at.c, at.z_at(offset)]
-        return remote(slab, slab, core_send.at[i], core_recv.at[i], other_core)
-
-    hops = ring_hops(Z)
-    ring = []
-    for n in range(X):
-        if n == 0:
-            q_own.wait()
-        else:
-            x_copies[n - 1].wait_recv()
-        for direction in range(2):
-            if (direction, 0) in hops:
-                copy = ring_copy(direction, 0, n)
-                copy.start()
-                ring.append(copy)
-    cores = [core_copy(0, 0)]
-    cores[0].start()
+        copy = remote(slab, slab, core_send.at[i], core_recv.at[i], other_core)
+        copy.start()
+        cores.append(copy)
 
     token = (at.ctx * sizes[1] + at.head) * tokens + lax.broadcasted_iota(jnp.int32, (tokens, HD), 0)
     first = jnp.zeros((tokens, HD), jnp.int32)
@@ -252,32 +241,34 @@
         k_copies.append(copy)
     ko[at.k] = turn(k_in[:, pl.ds(own, HD)], cosine, sine)
 
-    for step in range(Z // 2):
-        both = [direction for direction in range(2) if (direction, step) in hops]
+    for n in range(X):
+        for offset in (-1, 1):
+            arrived(offset, n)
+            pass_on(offset, n, -offset)
+    q_own.wait()
+    for n in range(1, X):
+        arrived(0, n)
+    for offset in (0, -1, 1):
+        to_core(offset)
+    for n in range(X):
+        for offset in (-2, 2):
+            arrived(offset, n)
+            if offset == -2:
+                pass_on(offset, n, 2)
+            pass_on(offset, n, -offset // 2)
+    for offset in (-2, 2):
+        to_core(offset)
+    for offset in (-3, 3, -4):
         for n in range(X):
-            for direction in both:
-                arrived(direction, step, n)
-                if (direction, step + 1) in hops:
-                    copy = ring_copy(direction, step + 1, n)
-                    copy.start()
-                    ring.append(copy)
-        for direction in both:
-            i = hops.index((direction, step))
-            copy = core_copy(i + 1, -(step + 1) if direction == 0 else step + 1)
-            copy.start()
-            cores.append(copy)
-
-    for i in range(Z):
-        if i == 0:
-            offset = 0
-        else:
-            direction, step = hops[i - 1]
-            offset = (step + 1) if direction == 0 else -(step + 1)
-        slab = qo.at[1 - at.c, at.z_at(offset)]
+            arrived(offset, n)
+        to_core(offset)
+
+    for i, offset in enumerate(slabs):
+        slab = qo.at[1 - at.c, at.z_at(-offset)]
         remote(slab, slab, core_send.at[i], core_recv.at[i], other_core).wait_recv()
     for copy in v_copies + k_copies + pair_copies:
         copy.wait_recv()
-    for copy in v_copies + k_copies + pair_copies + x_copies + ring + cores:
+    for copy in v_copies + k_copies + pair_copies + first_copies + onward + cores:
         copy.wait_send()
     v_own.wait()
     sv_copy.wait()
@@ -361,8 +352,7 @@
         return add_block(counts, b, cache_at, first, tokens, far, 0)
 
     counts = lax.fori_loop(0, blocks, cache_block, (jnp.int32(1), jnp.int32(1)))
-    mate = at.pair * 3 + (1 - at.hb) * (1 - 2 * at.pair)
-    first = (jnp.where(at.c == 0, at.x, mate) * Z + at.z) * rows
+    first = (jnp.where(at.c == 0, at.x, at.mate) * Z + at.z) * rows
     _, count = add_block(counts, jnp.int32(blocks), span_at, first, rows, -first, first)
     for i in range(4):
         e_group[count + i], e_chunk[count + i] = jnp.int32(0), jnp.int32(0)
@@ -441,10 +431,11 @@
 
 def reduce_kernel(
     sizes, part_hbm, stat_hbm, out_ref,
-    part_ref, stat_ref, cr, cr_stat, sb, sb_stat, rb, rb_stat, fb, fb_stat, xr, xr_stat,
+    part_ref, stat_ref, cr, cr_stat, sb, sb_stat, rb, rb_stat, fb, fb_stat, xr, xr_stat, factor_ref,
     core_send, core_recv, core_stat_send, core_stat_recv,
     ring_send, ring_recv, ring_stat_send, ring_stat_recv,
-    x_send, x_recv, x_stat_send, x_stat_recv, out_send, out_recv, own_sem, in_sem,
+    x_send, x_recv, x_stat_send, x_stat_recv, out_send, out_recv, cross_send, cross_recv, own_sem,
+    in_sem,
 ):
     at = Place(*sizes)
     Y, Z = at.Y, at.Z
@@ -455,28 +446,15 @@
     ]
     for copy in reads:
         copy.start()
-    others = [at.dev(x=(at.x + dx) % X) for dx in range(1, X)]
-    plus, minus = at.along_z(1), at.along_z(-1)
     other_core = at.dev(c=1 - at.c)
-    ends = [
-        at.dev(y=(at.y + dy) % Y, c=(at.c + dc) % 2)
-        for dc in range(2)
-        for dy in range(Y)
-        if dy or dc
-    ]
-    greet = others + ends + [plus]
-    if Z > 2:
-        greet.append(minus)
-    barrier(greet)
-
-    hops = ring_hops(Z)
-
-    def slab_offset(direction, step):
-        return Z // 2 - step if direction == 0 else -(Z // 2 - 1 - step)
-
-    offsets = [slab_offset(*hop) for hop in hops] + [0]
+    around = at.around()
+    ends = [at.dev(y=(at.y + dy) % Y) for dy in range(1, Y)]
+    greet = [device for _, _, device in around] + ends
+    barrier(greet + [at.along_z(2), at.along_z(-2), other_core])
+
+    slabs = (4, 3, -3, 2, -2, 1, -1, 0)
     sent = []
-    for i, offset in enumerate(offsets):
+    for i, offset in enumerate(slabs):
         z = at.z_at(-offset)
         a = remote(
             stat_hbm.at[1 - at.c, z], cr_stat.at[z], core_stat_send.at[i], core_stat_recv.at[i],
@@ -487,139 +465,174 @@
         b.start()
         sent += [a, b]
 
-    def from_core(i, offset):
-        z = at.z_at(offset)
+    def both_cores(offset):
+        i, z = slabs.index(offset), at.z_at(offset)
         remote(
             stat_ref.at[z], cr_stat.at[z], core_stat_send.at[i], core_stat_recv.at[i], other_core
         ).wait_recv()
-        remote(
-            part_ref.at[z], cr.at[z], core_send.at[i], core_recv.at[i], other_core
-        ).wait_recv()
+        remote(part_ref.at[z], cr.at[z], core_send.at[i], core_recv.at[i], other_core).wait_recv()
         return [(part_ref.at[z], stat_ref.at[z]), (cr.at[z], cr_stat.at[z])]
 
-    def ring_in(direction, step, x):
+    def ring_in(n, x):
         if x is None:
             remote(
-                sb_stat.at[direction, step], rb_stat.at[direction, step],
-                ring_stat_send.at[direction, step], ring_stat_recv.at[direction, step], plus,
+                sb_stat.at[n], rb_stat.at[n], ring_stat_send.at[n], ring_stat_recv.at[n], other_core
             ).wait_recv()
         else:
             remote(
-                sb.at[direction, step, x], rb.at[direction, step, x],
-                ring_send.at[direction, step, x], ring_recv.at[direction, step, x], plus,
+                sb.at[n, x], rb.at[n, x], ring_send.at[n, x], ring_recv.at[n, x], other_core
             ).wait_recv()
 
-    def join(sources, came, to, to_stat, emit):
-        for direction, step in came:
-            ring_in(direction, step, None)
-            sources = sources + [(rb.at[direction, step], rb_stat.at[direction, step])]
+    def ring_out(n, device):
+        def emit(x):
+            if x is None:
+                copy = remote(
+                    sb_stat.at[n], rb_stat.at[n], ring_stat_send.at[n], ring_stat_recv.at[n], device
+                )
+            else:
+                copy = remote(
+                    sb.at[n, x], rb.at[n, x], ring_send.at[n, x], ring_recv.at[n, x], device
+                )
+            copy.start()
+            sent.append(copy)
+
+        return emit
+
+    def join(sources, came, to, to_stat, emit, hold=None):
+        for n in came:
+            ring_in(n, None)
+            sources = sources + [(rb.at[n], rb_stat.at[n])]
         stats = [stat[...] for _, stat in sources]
         top = functools.reduce(jnp.maximum, [s[:X] for s in stats])
         factors = [jnp.exp2(s[:X] - top) for s in stats]
         to_stat[:X, :] = top
         to_stat[X:, :] = sum(s[X:] * f for s, f in zip(stats, factors))
         emit(None)
+        if hold is not None:
+            for i, f in enumerate(factors):
+                hold[i] = f
+
+        def factor(i, x):
+            return factors[i][x : x + 1] if hold is None else hold[i, pl.ds(x, 1), :]
 
         def piece(x):
-            for direction, step in came:
-                ring_in(direction, step, x)
+            for n in came:
+                ring_in(n, x)
             to[x] = sum(
-                part[x].astype(jnp.float32) * f[x : x + 1] for (part, _), f in zip(sources, factors)
+                part[x].astype(jnp.float32) * factor(i, x) for i, (part, _) in enumerate(sources)
             ).astype(jnp.bfloat16)
             emit(x)
 
         return piece
 
-    def ring_out(direction, step):
-        device = plus if direction == 0 else minus
-
-        def emit(x):
-            if x is None:
-                copy = remote(
-                    sb_stat.at[direction, step], rb_stat.at[direction, step],
-                    ring_stat_send.at[direction, step], ring_stat_recv.at[direction, step], device,
-                )
-            else:
-                copy = remote(
-                    sb.at[direction, step, x], rb.at[direction, step, x],
-                    ring_send.at[direction, step, x], ring_recv.at[direction, step, x], device,
-                )
-            copy.start()
-            sent.append(copy)
-
-        return emit
-
     for copy in reads:
         copy.wait()
-    for step in range(Z // 2):
+    stages = (
+        ((4, 2, 0, ()), (3, 1, 1, ()), (-3, -1, 2, ())),
+        ((2, 1, 3, (0, 1)), (-2, -1, 4, (2,))),
+    )
+    for stage in stages:
         pieces = [
             join(
-                from_core(i, slab_offset(*hop)), [(hop[0], step - 1)] if step else [],
-                sb.at[hop[0], step], sb_stat.at[hop[0], step], ring_out(*hop),
+                both_cores(offset), came, sb.at[n], sb_stat.at[n], ring_out(n, at.along_z(far))
             )
-            for i, hop in enumerate(hops)
-            if hop[1] == step
+            for offset, far, n, came in stage
         ]
         for x in range(X):
             for piece in pieces:
                 piece(x)
 
-    came = [(0, Z // 2 - 1)] + ([(1, Z // 2 - 2)] if Z > 2 else [])
-    piece = join(from_core(Z - 1, 0), came, fb, fb_stat, lambda x: None)
-    x_copies = []
-    for dx in range(1, X):
-        copy = remote(
-            fb_stat, xr_stat.at[at.x], x_stat_send.at[dx], x_stat_recv.at[dx], others[dx - 1]
-        )
-        copy.start()
-        x_copies.append(copy)
-    for x in range(X):
-        piece(x)
-    for dx in range(1, X):
-        x = (at.x + dx) % X
-        copy = remote(fb.at[x], xr.at[at.x], x_send.at[dx], x_recv.at[dx], others[dx - 1])
-        copy.start()
-        x_copies.append(copy)
-    sent += x_copies
-    own = [
-        pltpu.make_async_copy(fb.at[at.x], xr.at[at.x], own_sem.at[0]),
-        pltpu.make_async_copy(fb_stat, xr_stat.at[at.x], own_sem.at[1]),
-    ]
-    for copy in own:
-        copy.start()
+    def column_out(dz):
+        def emit(x):
+            for dx in range(X):
+                if (dz or dx) and x is None:
+                    copy = remote(
+                        fb_stat.at[dz + 1], xr_stat.at[-dz + 1, at.x], x_stat_send.at[dz + 1, dx],
+                        x_stat_recv.at[-dz + 1, dx], at.dev(x=(at.x + dx) % X, z=at.z_at(dz)),
+                    )
+                    copy.start()
+                    sent.append(copy)
+
+        return emit
+
+    own = []
+    for last in ((0,), (1, -1)):
+        pieces = [
+            join(
+                both_cores(dz), {0: (), 1: (3,), -1: (4,)}[dz], fb.at[dz + 1], fb_stat.at[dz + 1],
+                column_out(dz), factor_ref.at[dz + 1],
+            )
+            for dz in last
+        ]
+        for dx in range(X):
+            for dz, piece in zip(last, pieces):
+                x = (at.x + dx) % X
+                piece(x)
+                if dz or dx:
+                    copy = remote(
+                        fb.at[dz + 1, x], xr.at[-dz + 1, at.x], x_send.at[dz + 1, dx],
+                        x_recv.at[-dz + 1, dx], at.dev(x=x, z=at.z_at(dz)),
+                    )
+                    copy.start()
+                    sent.append(copy)
+                else:
+                    own = [
+                        pltpu.make_async_copy(fb.at[1, at.x], xr.at[1, at.x], own_sem.at[0]),
+                        pltpu.make_async_copy(fb_stat.at[1], xr_stat.at[1, at.x], own_sem.at[1]),
+                    ]
+                    for copy in own:
+                        copy.start()
     for copy in own:
         copy.wait()
-    for copy in x_copies:
-        copy.wait_recv()
-
-    outs = []
-    for hb, (one, two) in enumerate(((0, 3), (1, 2))):
-        tops = [xr_stat[n, pl.ds(at.x, 1), :] for n in (one, two)]
-        totals = [xr_stat[n, pl.ds(X + at.x, 1), :] for n in (one, two)]
-        top = jnp.maximum(*tops)
+    for dz in (0, 1, -1):
+        for dx in range(X):
+            if dz or dx:
+                remote(
+                    fb_stat.at[0], xr_stat.at[dz + 1, at.x], x_stat_send.at[dz + 1, dx],
+                    x_stat_recv.at[dz + 1, dx], other_core,
+                ).wait_recv()
+                remote(
+                    fb.at[0, 0], xr.at[dz + 1, at.x], x_send.at[dz + 1, dx], x_recv.at[dz + 1, dx],
+                    other_core,
+                ).wait_recv()
+
+    def columns(y, hb, c):
+        first = pl.multiple_of((2 * y + hb) * (GROUP * HD) + c * (2 * HD), 2 * HD)
+        return out_ref.at[:, pl.ds(first, 2 * HD)]
+
+    def cross(hb, dy):
+        part = columns((at.y - dy + Y) % Y, hb, at.c)
+        copy = remote(part, part, cross_send.at[hb, dy], cross_recv.at[hb, dy], other_core)
+        copy.start()
+        sent.append(copy)
+
+    for hb, pair in enumerate(((0, 3), (1, 2))):
+        sources = [(d, n) for n in pair for d in range(3)]
+        tops = [xr_stat[d, n, pl.ds(at.x, 1), :] for d, n in sources]
+        totals = [xr_stat[d, n, pl.ds(X + at.x, 1), :] for d, n in sources]
+        top = functools.reduce(jnp.maximum, tops)
         factors = [jnp.exp2(t - top) for t in tops]
-        total = totals[0] * factors[0] + totals[1] * factors[1]
-        value = xr[one].astype(jnp.float32) * factors[0] + xr[two].astype(jnp.float32) * factors[1]
+        total = sum(t * f for t, f in zip(totals, factors))
+        value = sum(xr[d, n].astype(jnp.float32) * f for (d, n), f in zip(sources, factors))
         value = (value / total).T.astype(jnp.bfloat16)
+        part = columns(at.y, hb, at.c)
         for h in range(2):
-            column = pl.multiple_of((2 * at.y + hb) * (GROUP * HD) + at.c * (2 * HD) + h * HD, HD)
-            out_ref[:, pl.ds(column, HD)] = value[h * rows : (h + 1) * rows]
-        column = pl.multiple_of((2 * at.y + hb) * (GROUP * HD) + at.c * (2 * HD), 2 * HD)
-        part = out_ref.at[:, pl.ds(column, 2 * HD)]
-        for i, device in enumerate(ends):
-            copy = remote(part, part, out_send.at[hb, i], out_recv.at[hb, i], device)
+            part[:, h * HD : (h + 1) * HD] = value[h * rows : (h + 1) * rows]
+        for dy in range(1, Y):
+            copy = remote(part, part, out_send.at[hb, dy], out_recv.at[hb, dy], ends[dy - 1])
             copy.start()
             sent.append(copy)
+        cross(hb, 0)
+    near = sorted(range(1, Y), key=lambda dy: min(dy, Y - dy))
     for hb in range(2):
-        i = 0
-        for dc in range(2):
-            for dy in range(Y):
-                if dy or dc:
-                    y, c = (at.y - dy + Y) % Y, (at.c - dc + 2) % 2
-                    column = pl.multiple_of((2 * y + hb) * (GROUP * HD) + c * (2 * HD), 2 * HD)
-                    part = out_ref.at[:, pl.ds(column, 2 * HD)]
-                    remote(part, part, out_send.at[hb, i], out_recv.at[hb, i], other_core).wait_recv()
-                    i += 1
+        for dy in near:
+            part = columns((at.y - dy + Y) % Y, hb, at.c)
+            remote(part, part, out_send.at[hb, dy], out_recv.at[hb, dy], other_core).wait_recv()
+            cross(hb, dy)
+    for hb in range(2):
+        for dy in range(Y):
+            part = columns((at.y - dy + Y) % Y, hb, 1 - at.c)
+            remote(part, part, cross_send.at[hb, dy], cross_recv.at[hb, dy], other_core).wait_recv()
     for copy in sent:
         copy.wait_send()
 
@@ -635,7 +648,6 @@
     hbm = pl.BlockSpec(memory_space=pltpu.HBM)
     dma = pltpu.SemaphoreType.DMA
     freq = jnp.asarray(inverse_freq())
-    half = Z // 2
 
     q_all, k_all, v_all, sk, sv = pl.pallas_call(
         functools.partial(gather_kernel, sizes),
@@ -656,7 +668,7 @@
             VMEM((rows, HD), bf16),
             VMEM((heads - 1, tokens, HD), bf16),
             dma((4,)), dma((2,)), dma((3,)), dma((heads,)), dma((heads,)), dma((heads,)), dma((heads,)),
-            dma((X,)), dma((X,)), dma((2, half, X)), dma((2, half, X)), dma((Z,)), dma((Z,)),
+            dma((3, X)), dma((Z, X)), dma((5 * X,)), dma((Z,)), dma((Z,)),
             dma((2,)), dma((2,)), dma((2,)),
         ],
         compiler_params=pltpu.CompilerParams(
@@ -702,14 +714,15 @@
         scratch_shapes=[
             VMEM((Z, X) + piece, bf16), VMEM((Z,) + stat, f32),
             VMEM((Z, X) + piece, bf16), VMEM((Z,) + stat, f32),
-            VMEM((2, half, X) + piece, bf16), VMEM((2, half) + stat, f32),
-            VMEM((2, half, X) + piece, bf16), VMEM((2, half) + stat, f32),
-            VMEM((X,) + piece, bf16), VMEM(stat, f32),
-            VMEM((X,) + piece, bf16), VMEM((X,) + stat, f32),
+            VMEM((5, X) + piece, bf16), VMEM((5,) + stat, f32),
+            VMEM((5, X) + piece, bf16), VMEM((5,) + stat, f32),
+            VMEM((3, X) + piece, bf16), VMEM((3,) + stat, f32),
+            VMEM((3, X) + piece, bf16), VMEM((3, X) + stat, f32),
+            VMEM((3, 3, X, 2 * rows), f32),
             dma((Z,)), dma((Z,)), dma((Z,)), dma((Z,)),
-            dma((2, half, X)), dma((2, half, X)), dma((2, half)), dma((2, half)),
-            dma((X,)), dma((X,)), dma((X,)), dma((X,)),
-            dma((2, 2 * Y)), dma((2, 2 * Y)), dma((2,)), dma((2,)),
+            dma((5, X)), dma((5, X)), dma((5,)), dma((5,)),
+            dma((3, X)), dma((3, X)), dma((3, X)), dma((3, X)),
+            dma((2, Y)), dma((2, Y)), dma((2, Y)), dma((2, Y)), dma((2,)), dma((2,)),
         ],
         compiler_params=pltpu.CompilerParams(
             collective_id=1, has_side_effects=True, vmem_limit_bytes=60 * 1024 * 1024

time: 80 us -> 76.9 us (0.961)
  Pallas kernels: 77.9 us -> 74.8 us
    pallas_call x1, Pallas kernels: 38.5 us -> 35.3 us  [body(): pl.pallas_call(functools.partial(gather_kernel, sizes), out_shape=(jax.Sh...]
    pallas_call x1, Pallas kernels: 31.5 us -> 32.6 us  [body(): pl.pallas_call(functools.partial(reduce_kernel, sizes), out_shape=jax.Sha...]
    pallas_call x1, Pallas kernels: 7.95 us -> 6.9 us  [body(): pl.pallas_call(functools.partial(attend_kernel, sizes), out_shape=(jax.Sh...]
where the time goes in v3:
time: 76.9 us; the launch traced here: 76.7 us
  Pallas kernels  74.8 us (97%)
  local copies, waits for them, and re-layouts  1.87 us (2%)
    pallas_call x1, Pallas kernels, body(): pl.pallas_call(functools.partial(gather_kernel, sizes), out_shape=(jax.Sh...  35.3 us
    pallas_call x1, Pallas kernels, body(): pl.pallas_call(functools.partial(reduce_kernel, sizes), out_shape=jax.Sha...  32.6 us
    pallas_call x1, Pallas kernels, body(): pl.pallas_call(functools.partial(attend_kernel, sizes), out_shape=(jax.Sh...  6.9 us
    unnamed x1, local copies, waits for them, and re-layouts  1.87 us

profile of v3, /device:TPU:1, one launch (start us, length us, event | category | flops | bytes accessed | tf_op | source)
XLA Modules:
  0.0 76.7 jit_solution(6976674988894308133)
XLA Ops:
  0.0 35.3 %gather.1 = (bf16[2,8,4,128,128]{4,3,2,1,0:T(8,128)(2,1)}, bf16[8,256,128]{2,1,0:T(8,128)(2,1)}, bf16[8,256,128]{2,1,0:T(8,128)(2,1)}, bf16[2,64,128]{2,1,0:T(8,128)(2,1)}, bf16[2,64,128]{2,1,0:T(8,128)(2,1)}) custom-call(s32[16]{0:T(128)} %cl_ref.3, s32[16]{0:T(128)} %sl_ref.3, f32[1,128]{1,0:T(1,128)} %constant.2.clone.freq_ref, bf16[64,4096]{1,0:T(8,128)(2,1)} %q_ref.1, ...), custom_call_target="tpu_custom_call" | custom-call | tf_op jit(solution)/shard_map/gather/pallas_call | solution.py:652
  35.3 6.9 %attend.1 = (bf16[2,8,4,128,128]{4,3,2,1,0:T(8,128)(2,1)}, f32[2,8,8,128]{3,2,1,0:T(8,128)}) custom-call(s32[16]{0:T(128)} %cl_ref.3, s32[16]{0:T(128)} %sl_ref.3, bf16[2,8,4,128,128]{4,3,2,1,0:T(8,128)(2,1)} %get-tuple-element.12.q_hbm, bf16[8,256,128]{2,1,0:T(8,128)(2,1)} %get-tuple-element.13.k_hbm, bf16[8,256,128]{2,1,0:T(8,128)(2,1)} %get-tuple-element.14.v_hbm, ...), custom_call_target="tpu_custom_call" | custom-call | tf_op jit(solution)/shard_map/attend/pallas_call | solution.py:687
  42.2 32.6 %reduce.1 = bf16[64,4096]{1,0:T(8,128)(2,1)} custom-call(bf16[2,8,4,128,128]{4,3,2,1,0:T(8,128)(2,1)} %get-tuple-element.17.part_hbm, f32[2,8,8,128]{3,2,1,0:T(8,128)} %get-tuple-element.18.stat_hbm), custom_call_target="tpu_custom_call" | custom-call | tf_op jit(solution)/shard_map/reduce/pallas_call | solution.py:709
  74.8 1.9 %copy.10 = bf16[64,4096]{1,0:T(8,128)(2,1)} copy(bf16[64,4096]{1,0:T(8,128)(2,1)} %reduce.1) | data formatting | bytes 1048576

commit v4 on v3

--- a/solution.py
+++ b/solution.py
@@ -105,9 +105,9 @@
 def gather_kernel(
     sizes, cl_ref, sl_ref, freq_ref, q_ref, sk_ref, sv_ref, k_ref, v_ref,
     qo, ko, vo, sko, svo,
-    cl, sl, freq_in, k_in, q_in, sk_in, qs, sks, ks, in_sem,
+    cl, sl, freq_in, k_in, q_in, sk_in, qs, qb, sks, ks, in_sem,
     q_in_sem, span_sem, v_send, v_recv, k_send, k_recv, q_send, q_recv, on_send,
-    core_send, core_recv, own_sem, pair_send, pair_recv,
+    core_send, core_recv, own_sem, q_own_sem, pair_send, pair_recv,
 ):
     at = Place(*sizes)
     Y, Z = at.Y, at.Z
@@ -147,17 +147,6 @@
     greet += [device for _, _, device in around] + [at.along_z(2), at.along_z(-2), other_core]
     barrier(greet)
 
-    order = sorted(range(1, heads), key=lambda d: -min(d, heads - d))
-    v_copies = []
-    for d in order:
-        k, device = partners[d - 1]
-        column = pl.multiple_of(k * HD, HD)
-        copy = remote(
-            v_ref.at[:, pl.ds(column, HD)], vo.at[at.k], v_send.at[d], v_recv.at[d], device
-        )
-        copy.start()
-        v_copies.append(copy)
-
     for copy in reads:
         copy.wait()
     freq = freq_in[...]
@@ -173,33 +162,34 @@
             qs[hb, h * rows : (h + 1) * rows, :] = turn(
                 q_in[hb, :, h * HD : (h + 1) * HD], cosine, sine
             )
-    sko[0] = turn(sk_in[0], cosine, sine)
-    sks[...] = turn(sk_in[1], cosine, sine)
-
-    q_own = pltpu.make_async_copy(qs.at[at.hb], qo.at[at.c, at.z, at.x], own_sem.at[1])
+    for i in range(2):
+        sks[i] = turn(sk_in[i], cosine, sine)
+
+    q_own = pltpu.make_async_copy(qs.at[at.hb], qb.at[at.z, at.x], own_sem.at[1])
     q_own.start()
     first_copies = []
     for dz, dx, device in around:
         copy = remote(
-            qs.at[at.bit_of((at.x + dx) % X)], qo.at[at.c, at.z, at.x],
+            qs.at[at.bit_of((at.x + dx) % X)], qb.at[at.z, at.x],
             q_send.at[dz + 1, dx], q_recv.at[-dz + 4, dx], device,
         )
         copy.start()
         first_copies.append(copy)
     pair_copies = [
-        remote(sks, sko.at[1], pair_send.at[0], pair_recv.at[0], at.dev(x=at.mate)),
+        remote(sks.at[1], sko.at[1], pair_send.at[0], pair_recv.at[0], at.dev(x=at.mate)),
         remote(
             sv_ref.at[:, pl.ds(theirs, HD)], svo.at[1], pair_send.at[1], pair_recv.at[1],
             at.dev(x=at.mate),
         ),
     ]
-    for copy in pair_copies:
+    sk_own = pltpu.make_async_copy(sks.at[0], sko.at[0], own_sem.at[2])
+    for copy in pair_copies + [sk_own]:
         copy.start()
 
     onward = []
 
     def piece(offset, n):
-        return qo.at[at.c, at.z_at(offset), (at.x - n + X) % X]
+        return qb.at[at.z_at(offset), (at.x - n + X) % X]
 
     def arrived(offset, n):
         part = piece(offset, n)
@@ -214,14 +204,30 @@
         onward.append(copy)
 
     slabs = (0, -1, 1, -2, 2, -3, 3, -4)
-    cores = []
+    cores, kept = [], []
 
     def to_core(offset):
         i = slabs.index(offset)
-        slab = qo.at[at.c, at.z_at(offset)]
-        copy = remote(slab, slab, core_send.at[i], core_recv.at[i], other_core)
+        z = at.z_at(offset)
+        copy = remote(
+            qb.at[z], qo.at[at.c, z], core_send.at[i], core_recv.at[i], other_core
+        )
         copy.start()
         cores.append(copy)
+        copy = pltpu.make_async_copy(qb.at[z], qo.at[at.c, z], q_own_sem.at[i])
+        copy.start()
+        kept.append(copy)
+
+    order = sorted(range(1, heads), key=lambda d: -min(d, heads - d))
+    v_copies = []
+    for d in order:
+        k, device = partners[d - 1]
+        column = pl.multiple_of(k * HD, HD)
+        copy = remote(
+            v_ref.at[:, pl.ds(column, HD)], vo.at[at.k], v_send.at[d], v_recv.at[d], device
+        )
+        copy.start()
+        v_copies.append(copy)
 
     token = (at.ctx * sizes[1] + at.head) * tokens + lax.broadcasted_iota(jnp.int32, (tokens, HD), 0)
     first = jnp.zeros((tokens, HD), jnp.int32)
@@ -235,11 +241,13 @@
     for d in order:
         k, device = partners[d - 1]
         column = pl.multiple_of(k * HD, HD)
-        ks[d - 1] = turn(k_in[:, pl.ds(column, HD)], cosine, sine)
-        copy = remote(ks.at[d - 1], ko.at[at.k], k_send.at[d], k_recv.at[d], device)
+        ks[d] = turn(k_in[:, pl.ds(column, HD)], cosine, sine)
+        copy = remote(ks.at[d], ko.at[at.k], k_send.at[d], k_recv.at[d], device)
         copy.start()
         k_copies.append(copy)
-    ko[at.k] = turn(k_in[:, pl.ds(own, HD)], cosine, sine)
+    ks[0] = turn(k_in[:, pl.ds(own, HD)], cosine, sine)
+    k_own = pltpu.make_async_copy(ks.at[0], ko.at[at.k], own_sem.at[3])
+    k_own.start()
 
     for n in range(X):
         for offset in (-1, 1):
@@ -264,20 +272,22 @@
         to_core(offset)
 
     for i, offset in enumerate(slabs):
-        slab = qo.at[1 - at.c, at.z_at(-offset)]
-        remote(slab, slab, core_send.at[i], core_recv.at[i], other_core).wait_recv()
+        z = at.z_at(-offset)
+        remote(
+            qb.at[z], qo.at[1 - at.c, z], core_send.at[i], core_recv.at[i], other_core
+        ).wait_recv()
     for copy in v_copies + k_copies + pair_copies:
         copy.wait_recv()
     for copy in v_copies + k_copies + pair_copies + first_copies + onward + cores:
         copy.wait_send()
-    v_own.wait()
-    sv_copy.wait()
+    for copy in kept + [v_own, k_own, sk_own, sv_copy]:
+        copy.wait()
 
 
 def attend_kernel(
-    sizes, cl_ref, sl_ref, q_hbm, k_hbm, v_hbm, sk_hbm, sv_hbm, part_ref, stat_ref,
-    acc, cl, sl, q_ref, k_ref, v_ref, vt_ref, s_even, s_odd, w_odd, f_odd,
-    cache_at, span_at, g_block, g_low, g_high, g_first, g_end, g_causal, e_group, e_chunk, in_sem,
+    sizes, cl_ref, sl_ref, q_hbm, k_hbm, v_hbm, sk_hbm, sv_hbm, part_hbm, stat_ref,
+    part_ref, acc, cl, sl, q_ref, k_ref, v_ref, vt_ref, s_even, s_odd, w_odd, f_odd,
+    cache_at, span_at, g_block, g_low, g_high, g_first, g_end, g_causal, e_group, e_chunk, in_sem, out_sem,
 ):
     at = Place(*sizes)
     Z = at.Z
@@ -426,7 +436,22 @@
     steps = count // 2
     lax.fori_loop(0, steps, step, 0)
     update(2 * steps, product(2 * steps, w_odd[...]), f_odd[...])
-    part_ref[...] = acc[...].astype(jnp.bfloat16)
+
+    def leave(i):
+        c, z = i // Z, i % Z
+        return pltpu.make_async_copy(part_ref.at[c, z], part_hbm.at[c, z], out_sem.at[i])
+
+    def slab(i, carry):
+        part_ref[i // Z, i % Z] = acc[i // Z, i % Z].astype(jnp.bfloat16)
+        leave(i).start()
+        return carry
+
+    def left(i, carry):
+        leave(i).wait()
+        return carry
+
+    lax.fori_loop(0, 2 * Z, slab, 0)
+    lax.fori_loop(0, 2 * Z, left, 0)
 
 
 def reduce_kernel(
@@ -531,7 +556,7 @@
         ((4, 2, 0, ()), (3, 1, 1, ()), (-3, -1, 2, ())),
         ((2, 1, 3, (0, 1)), (-2, -1, 4, (2,))),
     )
-    for stage in stages:
+    def work(stage):
         pieces = [
             join(
                 both_cores(offset), came, sb.at[n], sb_stat.at[n], ring_out(n, at.along_z(far))
@@ -556,7 +581,8 @@
         return emit
 
     own = []
-    for last in ((0,), (1, -1)):
+
+    def finish(last):
         pieces = [
             join(
                 both_cores(dz), {0: (), 1: (3,), -1: (4,)}[dz], fb.at[dz + 1], fb_stat.at[dz + 1],
@@ -576,12 +602,17 @@
                     copy.start()
                     sent.append(copy)
                 else:
-                    own = [
+                    own.extend((
                         pltpu.make_async_copy(fb.at[1, at.x], xr.at[1, at.x], own_sem.at[0]),
                         pltpu.make_async_copy(fb_stat.at[1], xr_stat.at[1, at.x], own_sem.at[1]),
-                    ]
+                    ))
                     for copy in own:
                         copy.start()
+
+    work(stages[0])
+    finish((0,))
+    work(stages[1])
+    finish((1, -1))
     for copy in own:
         copy.wait()
     for dz in (0, 1, -1):
@@ -659,17 +690,18 @@
             jax.ShapeDtypeStruct((2, rows, HD), bf16),
         ),
         in_specs=[hbm] * 8,
-        out_specs=(vmem,) * 5,
+        out_specs=(hbm,) * 5,
         scratch_shapes=[
             lengths, lengths, VMEM(freq.shape, f32), VMEM((tokens, heads * HD), bf16),
             VMEM((2, rows, 2 * HD), bf16),
             VMEM((2, rows, HD), bf16),
             VMEM((2, 2 * rows, HD), bf16),
-            VMEM((rows, HD), bf16),
-            VMEM((heads - 1, tokens, HD), bf16),
+            VMEM((Z, X, 2 * rows, HD), bf16),
+            VMEM((2, rows, HD), bf16),
+            VMEM((heads, tokens, HD), bf16),
             dma((4,)), dma((2,)), dma((3,)), dma((heads,)), dma((heads,)), dma((heads,)), dma((heads,)),
             dma((3, X)), dma((Z, X)), dma((5 * X,)), dma((Z,)), dma((Z,)),
-            dma((2,)), dma((2,)), dma((2,)),
+            dma((4,)), dma((Z,)), dma((2,)), dma((2,)),
         ],
         compiler_params=pltpu.CompilerParams(
             collective_id=0, has_side_effects=True, vmem_limit_bytes=60 * 1024 * 1024
@@ -691,15 +723,16 @@
             jax.ShapeDtypeStruct((2, Z, 2 * X, 2 * rows), f32),
         ),
         in_specs=[hbm] * 7,
-        out_specs=(vmem, vmem),
+        out_specs=(hbm, vmem),
         scratch_shapes=[
+            VMEM((2, Z, X, HD, 2 * rows), bf16),
             VMEM((2, Z, X, HD, 2 * rows), f32), lengths, lengths, VMEM(q_all.shape, bf16),
             VMEM((heads + 1, tokens, HD), bf16), VMEM((heads + 1, tokens, HD), bf16),
             VMEM((heads + 1, HD, tokens), bf16),
             VMEM((tokens, 4 * rows), f32), VMEM((tokens, 4 * rows), f32),
             VMEM((tokens, 4 * rows), bf16), VMEM((1, 4 * rows), f32),
             numbers(ndoc + 1), numbers(ndoc + 1), *[numbers(groups)] * 6,
-            numbers(entries), numbers(entries), dma((7,)),
+            numbers(entries), numbers(entries), dma((7,)), dma((2 * Z,)),
         ],
         compiler_params=pltpu.CompilerParams(vmem_limit_bytes=60 * 1024 * 1024),
         name="attend",

time: 76.9 us -> 73.2 us (0.952)
  Pallas kernels: 74.8 us -> 71.1 us
    pallas_call x1, Pallas kernels: 35.3 us -> 29.2 us  [body(): pl.pallas_call(functools.partial(gather_kernel, sizes), out_shape=(jax.Sh...]
    pallas_call x1, Pallas kernels: 6.9 us -> 10.3 us  [body(): pl.pallas_call(functools.partial(attend_kernel, sizes), out_shape=(jax.Sh...]
    pallas_call x1, Pallas kernels: 32.6 us -> 31.6 us  [body(): pl.pallas_call(functools.partial(reduce_kernel, sizes), out_shape=jax.Sha...]
where the time goes in v4:
time: 73.2 us; the launch traced here: 73 us
  Pallas kernels  71.1 us (97%)
  local copies, waits for them, and re-layouts  1.87 us (3%)
    pallas_call x1, Pallas kernels, body(): pl.pallas_call(functools.partial(reduce_kernel, sizes), out_shape=jax.Sha...  31.6 us
    pallas_call x1, Pallas kernels, body(): pl.pallas_call(functools.partial(gather_kernel, sizes), out_shape=(jax.Sh...  29.2 us
    pallas_call x1, Pallas kernels, body(): pl.pallas_call(functools.partial(attend_kernel, sizes), out_shape=(jax.Sh...  10.3 us
    unnamed x1, local copies, waits for them, and re-layouts  1.87 us

profile of v4, /device:TPU:1, one launch (start us, length us, event | category | flops | bytes accessed | tf_op | source)
XLA Modules:
  0.0 73.0 jit_solution(15875439653917460776)
XLA Ops:
  0.0 29.2 %gather.1 = (bf16[2,8,4,128,128]{4,3,2,1,0:T(8,128)(2,1)}, bf16[8,256,128]{2,1,0:T(8,128)(2,1)}, bf16[8,256,128]{2,1,0:T(8,128)(2,1)}, bf16[2,64,128]{2,1,0:T(8,128)(2,1)}, bf16[2,64,128]{2,1,0:T(8,128)(2,1)}) custom-call(s32[16]{0:T(128)} %cl_ref.3, s32[16]{0:T(128)} %sl_ref.3, f32[1,128]{1,0:T(1,128)} %constant.2.clone.freq_ref, bf16[64,4096]{1,0:T(8,128)(2,1)} %q_ref.1, ...), custom_call_target="tpu_custom_call" | custom-call | tf_op jit(solution)/shard_map/gather/pallas_call | solution.py:683
  29.2 10.3 %attend.1 = (bf16[2,8,4,128,128]{4,3,2,1,0:T(8,128)(2,1)}, f32[2,8,8,128]{3,2,1,0:T(8,128)}) custom-call(s32[16]{0:T(128)} %cl_ref.3, s32[16]{0:T(128)} %sl_ref.3, bf16[2,8,4,128,128]{4,3,2,1,0:T(8,128)(2,1)} %get-tuple-element.12.q_hbm, bf16[8,256,128]{2,1,0:T(8,128)(2,1)} %get-tuple-element.13.k_hbm, bf16[8,256,128]{2,1,0:T(8,128)(2,1)} %get-tuple-element.14.v_hbm, ...), custom_call_target="tpu_custom_call" | custom-call | tf_op jit(solution)/shard_map/attend/pallas_call | solution.py:719
  39.5 31.6 %reduce.1 = bf16[64,4096]{1,0:T(8,128)(2,1)} custom-call(bf16[2,8,4,128,128]{4,3,2,1,0:T(8,128)(2,1)} %get-tuple-element.17.part_hbm, f32[2,8,8,128]{3,2,1,0:T(8,128)} %get-tuple-element.18.stat_hbm), custom_call_target="tpu_custom_call" | custom-call | tf_op jit(solution)/shard_map/reduce/pallas_call | solution.py:742
  71.1 1.9 %copy.10 = bf16[64,4096]{1,0:T(8,128)(2,1)} copy(bf16[64,4096]{1,0:T(8,128)(2,1)} %reduce.1) | data formatting | bytes 1048576

commit v5 on v4

--- a/solution.py
+++ b/solution.py
@@ -285,9 +285,9 @@
 
 
 def attend_kernel(
-    sizes, cl_ref, sl_ref, q_hbm, k_hbm, v_hbm, sk_hbm, sv_hbm, part_hbm, stat_ref,
-    part_ref, acc, cl, sl, q_ref, k_ref, v_ref, vt_ref, s_even, s_odd, w_odd, f_odd,
-    cache_at, span_at, g_block, g_low, g_high, g_first, g_end, g_causal, e_group, e_chunk, in_sem, out_sem,
+    sizes, cl_ref, sl_ref, q_hbm, k_hbm, v_hbm, sk_hbm, sv_hbm, part_ref, stat_ref,
+    acc, cl, sl, q_ref, k_ref, v_ref, vt_ref, s_even, s_odd, w_odd, f_odd,
+    cache_at, span_at, g_block, g_low, g_high, g_first, g_end, g_causal, e_group, e_chunk, in_sem,
 ):
     at = Place(*sizes)
     Z = at.Z
@@ -436,27 +436,12 @@
     steps = count // 2
     lax.fori_loop(0, steps, step, 0)
     update(2 * steps, product(2 * steps, w_odd[...]), f_odd[...])
-
-    def leave(i):
-        c, z = i // Z, i % Z
-        return pltpu.make_async_copy(part_ref.at[c, z], part_hbm.at[c, z], out_sem.at[i])
-
-    def slab(i, carry):
-        part_ref[i // Z, i % Z] = acc[i // Z, i % Z].astype(jnp.bfloat16)
-        leave(i).start()
-        return carry
-
-    def left(i, carry):
-        leave(i).wait()
-        return carry
-
-    lax.fori_loop(0, 2 * Z, slab, 0)
-    lax.fori_loop(0, 2 * Z, left, 0)
+    part_ref[...] = acc[...].astype(jnp.bfloat16)
 
 
 def reduce_kernel(
-    sizes, part_hbm, stat_hbm, out_ref,
-    part_ref, stat_ref, cr, cr_stat, sb, sb_stat, rb, rb_stat, fb, fb_stat, xr, xr_stat, factor_ref,
+    sizes, part_hbm, stat_all, out_ref,
+    part_ref, cr, cr_stat, sb, sb_stat, rb, rb_stat, fb, fb_stat, xr, xr_stat, factor_ref,
     core_send, core_recv, core_stat_send, core_stat_recv,
     ring_send, ring_recv, ring_stat_send, ring_stat_recv,
     x_send, x_recv, x_stat_send, x_stat_recv, out_send, out_recv, cross_send, cross_recv, own_sem,
@@ -465,12 +450,9 @@
     at = Place(*sizes)
     Y, Z = at.Y, at.Z
     rows = out_ref.shape[0]
-    reads = [
-        pltpu.make_async_copy(stat_hbm.at[at.c], stat_ref, in_sem.at[0]),
-        pltpu.make_async_copy(part_hbm.at[at.c], part_ref, in_sem.at[1]),
-    ]
-    for copy in reads:
-        copy.start()
+    read = pltpu.make_async_copy(part_hbm.at[at.c], part_ref, in_sem.at[0])
+    read.start()
+    stat_ref = stat_all.at[at.c]
     other_core = at.dev(c=1 - at.c)
     around = at.around()
     ends = [at.dev(y=(at.y + dy) % Y) for dy in range(1, Y)]
@@ -478,23 +460,21 @@
     barrier(greet + [at.along_z(2), at.along_z(-2), other_core])
 
     slabs = (4, 3, -3, 2, -2, 1, -1, 0)
-    sent = []
+    stats_over = remote(
+        stat_all.at[1 - at.c], cr_stat, core_stat_send.at[0], core_stat_recv.at[0], other_core
+    )
+    stats_over.start()
+    sent = [stats_over]
     for i, offset in enumerate(slabs):
         z = at.z_at(-offset)
-        a = remote(
-            stat_hbm.at[1 - at.c, z], cr_stat.at[z], core_stat_send.at[i], core_stat_recv.at[i],
-            other_core,
+        copy = remote(
+            part_hbm.at[1 - at.c, z], cr.at[z], core_send.at[i], core_recv.at[i], other_core
         )
-        b = remote(part_hbm.at[1 - at.c, z], cr.at[z], core_send.at[i], core_recv.at[i], other_core)
-        a.start()
-        b.start()
-        sent += [a, b]
+        copy.start()
+        sent.append(copy)
 
     def both_cores(offset):
         i, z = slabs.index(offset), at.z_at(offset)
-        remote(
-            stat_ref.at[z], cr_stat.at[z], core_stat_send.at[i], core_stat_recv.at[i], other_core
-        ).wait_recv()
         remote(part_ref.at[z], cr.at[z], core_send.at[i], core_recv.at[i], other_core).wait_recv()
         return [(part_ref.at[z], stat_ref.at[z]), (cr.at[z], cr_stat.at[z])]
 
@@ -550,8 +530,8 @@
 
         return piece
 
-    for copy in reads:
-        copy.wait()
+    read.wait()
+    stats_over.wait_recv()
     stages = (
         ((4, 2, 0, ()), (3, 1, 1, ()), (-3, -1, 2, ())),
         ((2, 1, 3, (0, 1)), (-2, -1, 4, (2,))),
@@ -637,6 +617,7 @@
         copy.start()
         sent.append(copy)
 
+    near = sorted(range(1, Y), key=lambda dy: min(dy, Y - dy))
     for hb, pair in enumerate(((0, 3), (1, 2))):
         sources = [(d, n) for n in pair for d in range(3)]
         tops = [xr_stat[d, n, pl.ds(at.x, 1), :] for d, n in sources]
@@ -649,12 +630,11 @@
         part = columns(at.y, hb, at.c)
         for h in range(2):
             part[:, h * HD : (h + 1) * HD] = value[h * rows : (h + 1) * rows]
-        for dy in range(1, Y):
+        for dy in reversed(near):
             copy = remote(part, part, out_send.at[hb, dy], out_recv.at[hb, dy], ends[dy - 1])
             copy.start()
             sent.append(copy)
         cross(hb, 0)
-    near = sorted(range(1, Y), key=lambda dy: min(dy, Y - dy))
     for hb in range(2):
         for dy in near:
             part = columns((at.y - dy + Y) % Y, hb, at.c)
@@ -723,16 +703,15 @@
             jax.ShapeDtypeStruct((2, Z, 2 * X, 2 * rows), f32),
         ),
         in_specs=[hbm] * 7,
-        out_specs=(hbm, vmem),
+        out_specs=(vmem, vmem),
         scratch_shapes=[
-            VMEM((2, Z, X, HD, 2 * rows), bf16),
             VMEM((2, Z, X, HD, 2 * rows), f32), lengths, lengths, VMEM(q_all.shape, bf16),
             VMEM((heads + 1, tokens, HD), bf16), VMEM((heads + 1, tokens, HD), bf16),
             VMEM((heads + 1, HD, tokens), bf16),
             VMEM((tokens, 4 * rows), f32), VMEM((tokens, 4 * rows), f32),
             VMEM((tokens, 4 * rows), bf16), VMEM((1, 4 * rows), f32),
             numbers(ndoc + 1), numbers(ndoc + 1), *[numbers(groups)] * 6,
-            numbers(entries), numbers(entries), dma((7,)), dma((2 * Z,)),
+            numbers(entries), numbers(entries), dma((7,)),
         ],
         compiler_params=pltpu.CompilerParams(vmem_limit_bytes=60 * 1024 * 1024),
         name="attend",
@@ -742,23 +721,23 @@
     return pl.pallas_call(
         functools.partial(reduce_kernel, sizes),
         out_shape=jax.ShapeDtypeStruct(queries.shape, bf16),
-        in_specs=[hbm, hbm],
+        in_specs=[hbm, vmem],
         out_specs=vmem,
         scratch_shapes=[
-            VMEM((Z, X) + piece, bf16), VMEM((Z,) + stat, f32),
+            VMEM((Z, X) + piece, bf16),
             VMEM((Z, X) + piece, bf16), VMEM((Z,) + stat, f32),
             VMEM((5, X) + piece, bf16), VMEM((5,) + stat, f32),
             VMEM((5, X) + piece, bf16), VMEM((5,) + stat, f32),
             VMEM((3, X) + piece, bf16), VMEM((3,) + stat, f32),
             VMEM((3, X) + piece, bf16), VMEM((3, X) + stat, f32),
             VMEM((3, 3, X, 2 * rows), f32),
-            dma((Z,)), dma((Z,)), dma((Z,)), dma((Z,)),
+            dma((Z,)), dma((Z,)), dma((1,)), dma((1,)),
             dma((5, X)), dma((5, X)), dma((5,)), dma((5,)),
             dma((3, X)), dma((3, X)), dma((3, X)), dma((3, X)),
-            dma((2, Y)), dma((2, Y)), dma((2, Y)), dma((2, Y)), dma((2,)), dma((2,)),
+            dma((2, Y)), dma((2, Y)), dma((2, Y)), dma((2, Y)), dma((2,)), dma((1,)),
         ],
         compiler_params=pltpu.CompilerParams(
-            collective_id=1, has_side_effects=True, vmem_limit_bytes=60 * 1024 * 1024
+            collective_id=1, has_side_effects=True, vmem_limit_bytes=53 * 1024 * 1024
         ),
         name="reduce",
     )(parts, stats)

time: 73.2 us -> 73 us (level)
    pallas_call x1, Pallas kernels: 31.6 us -> 32.4 us  [body(): pl.pallas_call(functools.partial(reduce_kernel, sizes), out_shape=jax.Sha...]
    unnamed x1 -> x3, local copies, waits for them, and re-layouts: 1.87 us -> 1.63 us
where the time goes in v5:
time: 73 us; the launch traced here: 72.9 us
  Pallas kernels  71.2 us (98%)
  local copies, waits for them, and re-layouts  1.63 us (2%)
    pallas_call x1, Pallas kernels, body(): pl.pallas_call(functools.partial(reduce_kernel, sizes), out_shape=jax.Sha...  32.4 us
    pallas_call x1, Pallas kernels, body(): pl.pallas_call(functools.partial(gather_kernel, sizes), out_shape=(jax.Sh...  29.2 us
    pallas_call x1, Pallas kernels, body(): pl.pallas_call(functools.partial(attend_kernel, sizes), out_shape=(jax.Sh...  9.67 us
    unnamed x3, local copies, waits for them, and re-layouts  1.63 us

profile of v5, /device:TPU:1, one launch (start us, length us, event | category | flops | bytes accessed | tf_op | source)
XLA Modules:
  0.0 72.9 jit_solution(4712594643453106762)
XLA Ops:
  0.0 29.2 %gather.1 = (bf16[2,8,4,128,128]{4,3,2,1,0:T(8,128)(2,1)}, bf16[8,256,128]{2,1,0:T(8,128)(2,1)}, bf16[8,256,128]{2,1,0:T(8,128)(2,1)}, bf16[2,64,128]{2,1,0:T(8,128)(2,1)}, bf16[2,64,128]{2,1,0:T(8,128)(2,1)}) custom-call(s32[16]{0:T(128)} %cl_ref.3, s32[16]{0:T(128)} %sl_ref.3, f32[1,128]{1,0:T(1,128)} %constant.2.clone.freq_ref, bf16[64,4096]{1,0:T(8,128)(2,1)} %q_ref.1, ...), custom_call_target="tpu_custom_call" | custom-call | tf_op jit(solution)/shard_map/gather/pallas_call | solution.py:663
  29.2 9.7 %attend.1 = (bf16[2,8,4,128,128]{4,3,2,1,0:T(8,128)(2,1)}, f32[2,8,8,128]{3,2,1,0:T(8,128)}) custom-call(s32[16]{0:T(128)} %cl_ref.3, s32[16]{0:T(128)} %sl_ref.3, bf16[2,8,4,128,128]{4,3,2,1,0:T(8,128)(2,1)} %get-tuple-element.12.q_hbm, bf16[8,256,128]{2,1,0:T(8,128)(2,1)} %get-tuple-element.13.k_hbm, bf16[8,256,128]{2,1,0:T(8,128)(2,1)} %get-tuple-element.14.v_hbm, ...), custom_call_target="tpu_custom_call" | custom-call | tf_op jit(solution)/shard_map/attend/pallas_call | solution.py:699
  38.9 0.0 copy-start
  38.9 0.8 %copy-done = f32[2,8,8,128]{3,2,1,0:T(8,128)S(1)} copy-done((f32[2,8,8,128]{3,2,1,0:T(8,128)S(1)}, f32[2,8,8,128]{3,2,1,0:T(8,128)}, u32[]{:S(2)}) %copy-start) | copy-done | bytes 65560
  39.7 32.4 %reduce.1 = bf16[64,4096]{1,0:T(8,128)(2,1)S(1)} custom-call(bf16[2,8,4,128,128]{4,3,2,1,0:T(8,128)(2,1)} %get-tuple-element.17.part_hbm, f32[2,8,8,128]{3,2,1,0:T(8,128)S(1)} %copy-done), custom_call_target="tpu_custom_call" | custom-call | tf_op jit(solution)/shard_map/reduce/pallas_call | solution.py:721
  72.1 0.8 %copy.10 = bf16[64,4096]{1,0:T(8,128)(2,1)} copy(bf16[64,4096]{1,0:T(8,128)(2,1)S(1)} %reduce.1) | data formatting | bytes 1048576
Async XLA Ops:
  38.9 0.8 %copy-start = (f32[2,8,8,128]{3,2,1,0:T(8,128)S(1)}, f32[2,8,8,128]{3,2,1,0:T(8,128)}, u32[]{:S(2)}) copy-start(f32[2,8,8,128]{3,2,1,0:T(8,128)} %get-tuple-element.18.stat_all) | copy-start | bytes 196612

commit v6 on v5

--- a/solution.py
+++ b/solution.py
@@ -533,7 +533,8 @@
     read.wait()
     stats_over.wait_recv()
     stages = (
-        ((4, 2, 0, ()), (3, 1, 1, ()), (-3, -1, 2, ())),
+        ((4, 2, 0, ()),),
+        ((3, 1, 1, ()), (-3, -1, 2, ())),
         ((2, 1, 3, (0, 1)), (-2, -1, 4, (2,))),
     )
     def work(stage):
@@ -590,8 +591,9 @@
                         copy.start()
 
     work(stages[0])
+    work(stages[1])
     finish((0,))
-    work(stages[1])
+    work(stages[2])
     finish((1, -1))
     for copy in own:
         copy.wait()

time: 73 us -> 70.8 us (0.970)
  Pallas kernels: 71.2 us -> 69 us
    pallas_call x1, Pallas kernels: 32.4 us -> 29.7 us  [body(): pl.pallas_call(functools.partial(reduce_kernel, sizes), out_shape=jax.Sha...]
where the time goes in v6:
time: 70.8 us; the launch traced here: 70.6 us
  Pallas kernels  69 us (97%)
  local copies, waits for them, and re-layouts  1.63 us (2%)
    pallas_call x1, Pallas kernels, body(): pl.pallas_call(functools.partial(reduce_kernel, sizes), out_shape=jax.Sha...  29.7 us
    pallas_call x1, Pallas kernels, body(): pl.pallas_call(functools.partial(gather_kernel, sizes), out_shape=(jax.Sh...  29.2 us
    pallas_call x1, Pallas kernels, body(): pl.pallas_call(functools.partial(attend_kernel, sizes), out_shape=(jax.Sh...  10 us
    unnamed x3, local copies, waits for them, and re-layouts  1.63 us

profile of v6, /device:TPU:1, one launch (start us, length us, event | category | flops | bytes accessed | tf_op | source)
XLA Modules:
  0.0 70.6 jit_solution(11191034888017843894)
XLA Ops:
  0.0 29.2 %gather.1 = (bf16[2,8,4,128,128]{4,3,2,1,0:T(8,128)(2,1)}, bf16[8,256,128]{2,1,0:T(8,128)(2,1)}, bf16[8,256,128]{2,1,0:T(8,128)(2,1)}, bf16[2,64,128]{2,1,0:T(8,128)(2,1)}, bf16[2,64,128]{2,1,0:T(8,128)(2,1)}) custom-call(s32[16]{0:T(128)} %cl_ref.3, s32[16]{0:T(128)} %sl_ref.3, f32[1,128]{1,0:T(1,128)} %constant.2.clone.freq_ref, bf16[64,4096]{1,0:T(8,128)(2,1)} %q_ref.1, ...), custom_call_target="tpu_custom_call" | custom-call | tf_op jit(solution)/shard_map/gather/pallas_call | solution.py:665
  29.2 10.0 %attend.1 = (bf16[2,8,4,128,128]{4,3,2,1,0:T(8,128)(2,1)}, f32[2,8,8,128]{3,2,1,0:T(8,128)}) custom-call(s32[16]{0:T(128)} %cl_ref.3, s32[16]{0:T(128)} %sl_ref.3, bf16[2,8,4,128,128]{4,3,2,1,0:T(8,128)(2,1)} %get-tuple-element.12.q_hbm, bf16[8,256,128]{2,1,0:T(8,128)(2,1)} %get-tuple-element.13.k_hbm, bf16[8,256,128]{2,1,0:T(8,128)(2,1)} %get-tuple-element.14.v_hbm, ...), custom_call_target="tpu_custom_call" | custom-call | tf_op jit(solution)/shard_map/attend/pallas_call | solution.py:701
  39.3 0.0 copy-start
  39.3 0.8 %copy-done = f32[2,8,8,128]{3,2,1,0:T(8,128)S(1)} copy-done((f32[2,8,8,128]{3,2,1,0:T(8,128)S(1)}, f32[2,8,8,128]{3,2,1,0:T(8,128)}, u32[]{:S(2)}) %copy-start) | copy-done | bytes 65560
  40.1 29.7 %reduce.1 = bf16[64,4096]{1,0:T(8,128)(2,1)S(1)} custom-call(bf16[2,8,4,128,128]{4,3,2,1,0:T(8,128)(2,1)} %get-tuple-element.17.part_hbm, f32[2,8,8,128]{3,2,1,0:T(8,128)S(1)} %copy-done), custom_call_target="tpu_custom_call" | custom-call | tf_op jit(solution)/shard_map/reduce/pallas_call | solution.py:723
  69.8 0.8 %copy.10 = bf16[64,4096]{1,0:T(8,128)(2,1)} copy(bf16[64,4096]{1,0:T(8,128)(2,1)S(1)} %reduce.1) | data formatting | bytes 1048576
Async XLA Ops:
  39.3 0.8 %copy-start = (f32[2,8,8,128]{3,2,1,0:T(8,128)S(1)}, f32[2,8,8,128]{3,2,1,0:T(8,128)}, u32[]{:S(2)}) copy-start(f32[2,8,8,128]{3,2,1,0:T(8,128)} %get-tuple-element.18.stat_all) | copy-start | bytes 196612

commit v7 on v6

--- a/solution.py
+++ b/solution.py
@@ -285,9 +285,9 @@
 
 
 def attend_kernel(
-    sizes, cl_ref, sl_ref, q_hbm, k_hbm, v_hbm, sk_hbm, sv_hbm, part_ref, stat_ref,
-    acc, cl, sl, q_ref, k_ref, v_ref, vt_ref, s_even, s_odd, w_odd, f_odd,
-    cache_at, span_at, g_block, g_low, g_high, g_first, g_end, g_causal, e_group, e_chunk, in_sem,
+    sizes, cl_ref, sl_ref, q_hbm, k_hbm, v_hbm, sk_hbm, sv_hbm, part_ref, stat_hbm,
+    stat_ref, acc, cl, sl, q_ref, k_ref, v_ref, vt_ref, s_even, s_odd, w_odd, f_odd,
+    cache_at, span_at, g_block, g_low, g_high, g_first, g_end, g_causal, e_group, e_chunk, in_sem, out_sem,
 ):
     at = Place(*sizes)
     Z = at.Z
@@ -436,12 +436,15 @@
     steps = count // 2
     lax.fori_loop(0, steps, step, 0)
     update(2 * steps, product(2 * steps, w_odd[...]), f_odd[...])
+    leave = pltpu.make_async_copy(stat_ref, stat_hbm.at[pl.ds(0, 2)], out_sem.at[0])
+    leave.start()
     part_ref[...] = acc[...].astype(jnp.bfloat16)
+    leave.wait()
 
 
 def reduce_kernel(
-    sizes, part_hbm, stat_all, out_ref,
-    part_ref, cr, cr_stat, sb, sb_stat, rb, rb_stat, fb, fb_stat, xr, xr_stat, factor_ref,
+    sizes, part_hbm, stat_hbm, out_ref,
+    part_ref, stat_ref, cr, cr_stat, sb, sb_stat, rb, rb_stat, fb, fb_stat, xr, xr_stat, factor_ref,
     core_send, core_recv, core_stat_send, core_stat_recv,
     ring_send, ring_recv, ring_stat_send, ring_stat_recv,
     x_send, x_recv, x_stat_send, x_stat_recv, out_send, out_recv, cross_send, cross_recv, own_sem,
@@ -450,9 +453,12 @@
     at = Place(*sizes)
     Y, Z = at.Y, at.Z
     rows = out_ref.shape[0]
-    read = pltpu.make_async_copy(part_hbm.at[at.c], part_ref, in_sem.at[0])
-    read.start()
-    stat_ref = stat_all.at[at.c]
+    reads = [
+        pltpu.make_async_copy(stat_hbm.at[at.c], stat_ref, in_sem.at[0]),
+        pltpu.make_async_copy(part_hbm.at[at.c], part_ref, in_sem.at[1]),
+    ]
+    for copy in reads:
+        copy.start()
     other_core = at.dev(c=1 - at.c)
     around = at.around()
     ends = [at.dev(y=(at.y + dy) % Y) for dy in range(1, Y)]
@@ -461,7 +467,7 @@
 
     slabs = (4, 3, -3, 2, -2, 1, -1, 0)
     stats_over = remote(
-        stat_all.at[1 - at.c], cr_stat, core_stat_send.at[0], core_stat_recv.at[0], other_core
+        stat_hbm.at[1 - at.c], cr_stat, core_stat_send.at[0], core_stat_recv.at[0], other_core
     )
     stats_over.start()
     sent = [stats_over]
@@ -530,7 +536,8 @@
 
         return piece
 
-    read.wait()
+    for copy in reads:
+        copy.wait()
     stats_over.wait_recv()
     stages = (
         ((4, 2, 0, ()),),
@@ -702,18 +709,19 @@
         functools.partial(attend_kernel, sizes),
         out_shape=(
             jax.ShapeDtypeStruct((2, Z, X, HD, 2 * rows), bf16),
-            jax.ShapeDtypeStruct((2, Z, 2 * X, 2 * rows), f32),
+            jax.ShapeDtypeStruct((16, Z, 2 * X, 2 * rows), f32),
         ),
         in_specs=[hbm] * 7,
-        out_specs=(vmem, vmem),
+        out_specs=(vmem, hbm),
         scratch_shapes=[
+            VMEM((2, Z, 2 * X, 2 * rows), f32),
             VMEM((2, Z, X, HD, 2 * rows), f32), lengths, lengths, VMEM(q_all.shape, bf16),
             VMEM((heads + 1, tokens, HD), bf16), VMEM((heads + 1, tokens, HD), bf16),
             VMEM((heads + 1, HD, tokens), bf16),
             VMEM((tokens, 4 * rows), f32), VMEM((tokens, 4 * rows), f32),
             VMEM((tokens, 4 * rows), bf16), VMEM((1, 4 * rows), f32),
             numbers(ndoc + 1), numbers(ndoc + 1), *[numbers(groups)] * 6,
-            numbers(entries), numbers(entries), dma((7,)),
+            numbers(entries), numbers(entries), dma((7,)), dma((1,)),
         ],
         compiler_params=pltpu.CompilerParams(vmem_limit_bytes=60 * 1024 * 1024),
         name="attend",
@@ -723,10 +731,10 @@
     return pl.pallas_call(
         functools.partial(reduce_kernel, sizes),
         out_shape=jax.ShapeDtypeStruct(queries.shape, bf16),
-        in_specs=[hbm, vmem],
+        in_specs=[hbm, hbm],
         out_specs=vmem,
         scratch_shapes=[
-            VMEM((Z, X) + piece, bf16),
+            VMEM((Z, X) + piece, bf16), VMEM((Z,) + stat, f32),
             VMEM((Z, X) + piece, bf16), VMEM((Z,) + stat, f32),
             VMEM((5, X) + piece, bf16), VMEM((5,) + stat, f32),
             VMEM((5, X) + piece, bf16), VMEM((5,) + stat, f32),
@@ -736,7 +744,7 @@
             dma((Z,)), dma((Z,)), dma((1,)), dma((1,)),
             dma((5, X)), dma((5, X)), dma((5,)), dma((5,)),
             dma((3, X)), dma((3, X)), dma((3, X)), dma((3, X)),
-            dma((2, Y)), dma((2, Y)), dma((2, Y)), dma((2, Y)), dma((2,)), dma((1,)),
+            dma((2, Y)), dma((2, Y)), dma((2, Y)), dma((2, Y)), dma((2,)), dma((2,)),
         ],
         compiler_params=pltpu.CompilerParams(
             collective_id=1, has_side_effects=True, vmem_limit_bytes=53 * 1024 * 1024

time: 70.8 us -> 69.9 us (0.987)
  local copies, waits for them, and re-layouts: 1.63 us -> 0.8 us
    unnamed x3 -> x1, local copies, waits for them, and re-layouts: 1.63 us -> 0.8 us
where the time goes in v7:
time: 69.9 us
  Pallas kernels  69.1 us (99%)
  local copies, waits for them, and re-layouts  0.8 us (1%)
    pallas_call x1, Pallas kernels, body(): pl.pallas_call(functools.partial(reduce_kernel, sizes), out_shape=jax.Sha...  29.2 us
    pallas_call x1, Pallas kernels, body(): pl.pallas_call(functools.partial(gather_kernel, sizes), out_shape=(jax.Sh...  29.2 us
    pallas_call x1, Pallas kernels, body(): pl.pallas_call(functools.partial(attend_kernel, sizes), out_shape=(jax.Sh...  10.6 us

profile of v7, /device:TPU:1, one launch (start us, length us, event | category | flops | bytes accessed | tf_op | source)
XLA Modules:
  0.0 69.9 jit_solution(3455325767181170257)
XLA Ops:
  0.0 29.2 %gather.1 = (bf16[2,8,4,128,128]{4,3,2,1,0:T(8,128)(2,1)}, bf16[8,256,128]{2,1,0:T(8,128)(2,1)}, bf16[8,256,128]{2,1,0:T(8,128)(2,1)}, bf16[2,64,128]{2,1,0:T(8,128)(2,1)}, bf16[2,64,128]{2,1,0:T(8,128)(2,1)}) custom-call(s32[16]{0:T(128)} %cl_ref.3, s32[16]{0:T(128)} %sl_ref.3, f32[1,128]{1,0:T(1,128)} %constant.2.clone.freq_ref, bf16[64,4096]{1,0:T(8,128)(2,1)} %q_ref.1, ...), custom_call_target="tpu_custom_call" | custom-call | tf_op jit(solution)/shard_map/gather/pallas_call | solution.py:672
  29.2 10.6 %attend.1 = (bf16[2,8,4,128,128]{4,3,2,1,0:T(8,128)(2,1)}, f32[16,8,8,128]{3,2,1,0:T(8,128)}) custom-call(s32[16]{0:T(128)} %cl_ref.3, s32[16]{0:T(128)} %sl_ref.3, bf16[2,8,4,128,128]{4,3,2,1,0:T(8,128)(2,1)} %get-tuple-element.12.q_hbm, bf16[8,256,128]{2,1,0:T(8,128)(2,1)} %get-tuple-element.13.k_hbm, bf16[8,256,128]{2,1,0:T(8,128)(2,1)} %get-tuple-element.14.v_hbm, ...), custom_call_target="tpu_custom_call" | custom-call | tf_op jit(solution)/shard_map/attend/pallas_call | solution.py:708
  39.9 29.2 %reduce.1 = bf16[64,4096]{1,0:T(8,128)(2,1)S(1)} custom-call(bf16[2,8,4,128,128]{4,3,2,1,0:T(8,128)(2,1)} %get-tuple-element.17.part_hbm, f32[16,8,8,128]{3,2,1,0:T(8,128)} %get-tuple-element.18.stat_hbm), custom_call_target="tpu_custom_call" | custom-call | tf_op jit(solution)/shard_map/reduce/pallas_call | solution.py:731
  69.1 0.8 %copy.10 = bf16[64,4096]{1,0:T(8,128)(2,1)} copy(bf16[64,4096]{1,0:T(8,128)(2,1)S(1)} %reduce.1) | data formatting | bytes 1048576
